TPU v7x, 512 devices: a whole 4x4x16 slice. The times are simulated.
512 devices in a mesh: seq: 64 (over z, y), rep: 8 (over x, core).
Axes of the slice: x: 4, y: 4, z: 16, core: 2. Of those that a mesh axis runs over, the one named last changes fastest.
Arguments:
- queries: bfloat16 [8, 8192, 1024], P('rep', 'seq'), may hold values from -6.5 to 6.5
- keys: bfloat16 [8, 8192, 128], P('rep', 'seq'), may hold values from -4 to 4
- values: bfloat16 [8, 8192, 128], P('rep', 'seq'), may hold values from -5 to 5
- out_grad: bfloat16 [8, 8192, 1024], P('rep', 'seq'), may hold values from -5 to 5
- q_bias: float32 [1024], replicated, may hold values from -3 to 3
- v_bias: float32 [128], replicated, may hold values from -3 to 3
- doc_lengths: int32 [8, 16], P('rep'), may hold values from 1 to 897, 8192 in all within a row
Outputs:
- attended: bfloat16 [8, 8192, 1024], P('rep', 'seq')
- q_grad: float32 [8, 8192, 1024], P('rep', 'seq')
- k_grad: float32 [8, 8192, 128], P('rep', 'seq')
- v_grad: float32 [8, 8192, 128], P('rep', 'seq')
- q_bias_grad: float32 [1024], replicated
- v_bias_grad: float32 [128], replicated
Inputs may be any that keep to these rules, and one draw needn't show every extreme that they name: `doc_lengths`: each micro-batch holds 16 documents in order whose lengths sum to 8192; the longest is exactly 897 tokens.
All inputs are finite; a program needn't handle non-finite values.
Results may differ from a plain program's by a relative error of at most 0.04.
Values may be sent and summed in bfloat16 or wider, within the bound.
No kernel may reach another device: no remote copies, remote signals or barrier semaphores. Data moves between devices by JAX's collectives and lax.ppermute only.
A program may use at most 64 MiB of HBM per device.

v0:
```python
import math

import jax
import jax.numpy as jnp
from jax import lax
from jax.sharding import PartitionSpec as P

SPAN = 8


masked_fill = -1e30


def passed_along(block, axis, distance):
    devices = range(lax.axis_size(axis))
    route = [(i - distance, i) for i in devices if i - distance in devices]
    return lax.ppermute(block, axis, route)


def doc_index(doc_ends, positions):
    return jnp.sum((doc_ends[None, :] <= positions[:, None]).astype(jnp.int32), axis=1)


def allowed_mask(doc_ends, query_pos, key_pos):
    same_doc = doc_index(doc_ends, query_pos)[:, None] == doc_index(doc_ends, key_pos)[None, :]
    return same_doc & (key_pos[None, :] <= query_pos[:, None]) & (key_pos[None, :] >= 0)


def per_device(queries, keys, values, out_grad, q_bias, v_bias, doc_lengths):
    f32 = jnp.float32
    bf16 = jnp.bfloat16
    row_count = queries.shape[1]
    head_dim = keys.shape[2]
    head_count = queries.shape[2] // head_dim
    span_count = SPAN
    score_scale = 1.0 / math.sqrt(head_dim)
    shard_index = lax.axis_index("seq")
    query_pos = shard_index * row_count + jnp.arange(row_count, dtype=jnp.int32)
    doc_ends = jnp.cumsum(doc_lengths[0])
    query_rows = (
        (queries[0].astype(f32) + q_bias[None, :])
        .astype(bf16)
        .reshape(row_count, head_count, head_dim)
    )
    value_rows = (values[0].astype(f32) + v_bias[None, :]).astype(bf16)
    grad_rows = out_grad[0].reshape(row_count, head_count, head_dim)
    paired = jnp.concatenate([keys[0], value_rows], axis=1)
    collected = [paired]
    for distance in range(1, span_count):
        collected.append(passed_along(paired, "seq", distance))
    window = jnp.stack(collected)

    def block_mask(offset):
        key_pos = (shard_index - offset) * row_count + jnp.arange(row_count, dtype=jnp.int32)
        return allowed_mask(doc_ends, query_pos, key_pos)[None]

    def block_scores(offset):
        allowed = block_mask(offset)
        scores = (
            jnp.einsum(
                "thd,kd->htk", query_rows, window[offset, :, :head_dim], preferred_element_type=f32
            )
            * score_scale
        )
        return (allowed, jnp.where(allowed, scores, masked_fill))

    top = jnp.full((head_count, row_count, 1), masked_fill, f32)
    total = jnp.zeros((head_count, row_count, 1), f32)
    for offset in range(span_count):

        def partial_norm(offset=offset):
            allowed, scores = block_scores(offset)
            block_top = jnp.max(scores, axis=2, keepdims=True)
            block_sum = jnp.sum(
                jnp.where(allowed, jnp.exp(scores - block_top), 0.0), axis=2, keepdims=True
            )
            return (block_top, block_sum)

        block_top, block_sum = partial_norm()
        merged = jnp.maximum(top, block_top)
        total = total * jnp.exp(top - merged) + block_sum * jnp.exp(block_top - merged)
        top = merged
    log_norm = top + jnp.log(total)

    def block_weights(offset):
        allowed, scores = block_scores(offset)
        weights = jnp.where(allowed, jnp.exp(scores - log_norm), 0.0)
        return (weights, weights.astype(bf16))

    accum = jnp.zeros((row_count, head_count, head_dim), f32)
    for offset in range(span_count):

        def forward_part(offset=offset):
            weights, probs = block_weights(offset)
            return jnp.einsum(
                "htk,kd->thd", probs, window[offset, :, head_dim:], preferred_element_type=f32
            )

        accum = accum + forward_part()
    attended = accum.astype(bf16)
    delta = jnp.einsum("thd,thd->ht", grad_rows.astype(f32), attended.astype(f32))
    q_grad = jnp.zeros((row_count, head_count, head_dim), f32)
    partials = []
    for offset in range(span_count):

        def backward_part(offset=offset):
            weights, probs = block_weights(offset)
            key_block = window[offset, :, :head_dim]
            value_block = window[offset, :, head_dim:]
            d_probs = jnp.einsum("thd,kd->htk", grad_rows, value_block, preferred_element_type=f32)
            d_scores = (weights * (d_probs - delta[:, :, None]) * score_scale).astype(bf16)
            q_part = jnp.einsum("htk,kd->thd", d_scores, key_block, preferred_element_type=f32)
            k_term = jnp.einsum("htk,thd->kd", d_scores, query_rows, preferred_element_type=f32)
            v_term = jnp.einsum("htk,thd->kd", probs, grad_rows, preferred_element_type=f32)
            return (q_part, jnp.concatenate([k_term, v_term], axis=1))

        q_part, term_rows = backward_part()
        q_grad = q_grad + q_part
        partials.append(term_rows)
    owned = partials[0]
    for distance in range(1, span_count):
        owned = owned + passed_along(
            partials[distance].astype(jnp.bfloat16), "seq", -distance
        ).astype(jnp.float32)
    k_grad = owned[:, :head_dim]
    v_grad = owned[:, head_dim:]
    q_flat = q_grad.reshape(row_count, head_count * head_dim)
    q_sum = jnp.sum(q_flat, axis=0)
    v_sum = jnp.sum(v_grad, axis=0)
    q_total, v_total = lax.psum((q_sum, v_sum), ("seq", "rep"))
    token_total = lax.axis_size("seq") * row_count * lax.axis_size("rep")
    inverse = 1.0 / math.sqrt(token_total)
    return (
        attended.reshape(1, row_count, head_count * head_dim),
        q_flat[None],
        k_grad[None],
        v_grad[None],
        q_total * inverse,
        v_total * inverse,
    )


def solution(mesh):
    return jax.shard_map(
        per_device,
        mesh=mesh,
        in_specs=(
            P("rep", "seq", None),
            P("rep", "seq", None),
            P("rep", "seq", None),
            P("rep", "seq", None),
            P(),
            P(),
            P("rep", None),
        ),
        out_specs=(
            P("rep", "seq", None),
            P("rep", "seq", None),
            P("rep", "seq", None),
            P("rep", "seq", None),
            P(),
            P(),
        ),
        check_vma=False,
    )
```

profile of v0, /device:TPU:1, one launch (start us, length us, event | category | flops | bytes accessed | tf_op | source)
XLA Modules:
  0.0 209.7 jit_solution(8529360280688717517)
XLA Ops:
  2.1 4.0 %collective-permute-start = (bf16[128,256]{1,0:T(8,128)(2,1)}, bf16[128,256]{1,0:T(8,128)(2,1)S(1)}, u32[]{:S(2)}, u32[]{:S(2)}) collective-permute-start(bf16[128,256]{1,0:T(8,128)(2,1)} %get-tuple-element.38), channel_id=1, source_target_pairs={{0,8},{8,16},{16,24},{24,32},{32,40},{40,48},{48,56},{56,64},{64,7... | collective-permute-start | bytes 196616 | tf_op jit(solution)/shard_map/ppermute | solution.py:17
  6.2 4.6 %collective-permute-start.2 = (bf16[128,256]{1,0:T(8,128)(2,1)}, bf16[128,256]{1,0:T(8,128)(2,1)S(1)}, u32[]{:S(2)}, u32[]{:S(2)}) collective-permute-start(bf16[128,256]{1,0:T(8,128)(2,1)} %get-tuple-element.38), channel_id=1, source_target_pairs={{0,24},{8,32},{16,40},{24,48},{32,56},{40,64},{48,72},{56,80},{64,... | collective-permute-start | bytes 196616 | tf_op jit(solution)/shard_map/ppermute | solution.py:17
  10.8 3.5 %collective-permute-start.3 = (bf16[128,256]{1,0:T(8,128)(2,1)}, bf16[128,256]{1,0:T(8,128)(2,1)S(1)}, u32[]{:S(2)}, u32[]{:S(2)}) collective-permute-start(bf16[128,256]{1,0:T(8,128)(2,1)} %get-tuple-element.38), channel_id=1, source_target_pairs={{0,32},{8,40},{16,48},{24,56},{32,64},{40,72},{48,80},{56,88},{64,... | collective-permute-start | bytes 196616 | tf_op jit(solution)/shard_map/ppermute | solution.py:17
  14.4 3.6 %collective-permute-start.1 = (bf16[128,256]{1,0:T(8,128)(2,1)}, bf16[128,256]{1,0:T(8,128)(2,1)S(1)}, u32[]{:S(2)}, u32[]{:S(2)}) collective-permute-start(bf16[128,256]{1,0:T(8,128)(2,1)} %get-tuple-element.38), channel_id=1, source_target_pairs={{0,16},{8,24},{16,32},{24,40},{32,48},{40,56},{48,64},{56,72},{64,... | collective-permute-start | bytes 196616 | tf_op jit(solution)/shard_map/ppermute | solution.py:17
  18.0 4.3 %collective-permute-start.4 = (bf16[128,256]{1,0:T(8,128)(2,1)}, bf16[128,256]{1,0:T(8,128)(2,1)}, u32[]{:S(2)}, u32[]{:S(2)}) collective-permute-start(bf16[128,256]{1,0:T(8,128)(2,1)} %get-tuple-element.38), channel_id=1, source_target_pairs={{0,40},{8,48},{16,56},{24,64},{32,72},{40,80},{48,88},{56,96},{64,... | collective-permute-start | bytes 196616 | tf_op jit(solution)/shard_map/ppermute | solution.py:17
  26.9 6.8 %collective-permute-start.5 = (bf16[128,256]{1,0:T(8,128)(2,1)}, bf16[128,256]{1,0:T(8,128)(2,1)S(1)}, u32[]{:S(2)}, u32[]{:S(2)}) collective-permute-start(bf16[128,256]{1,0:T(8,128)(2,1)} %get-tuple-element.38), channel_id=1, source_target_pairs={{0,48},{8,56},{16,64},{24,72},{32,80},{40,88},{48,96},{56,104},{64... | collective-permute-start | bytes 196616 | tf_op jit(solution)/shard_map/ppermute | solution.py:17
  34.1 6.0 %collective-permute-start.6 = (bf16[128,256]{1,0:T(8,128)(2,1)}, bf16[128,256]{1,0:T(8,128)(2,1)S(1)}, u32[]{:S(2)}, u32[]{:S(2)}) collective-permute-start(bf16[128,256]{1,0:T(8,128)(2,1)} %get-tuple-element.38), channel_id=1, source_target_pairs={{0,56},{8,64},{16,72},{24,80},{32,88},{40,96},{48,104},{56,112},{6... | collective-permute-start | bytes 196616 | tf_op jit(solution)/shard_map/ppermute | solution.py:17
  47.8 1.0 fusion.106
  50.8 1.2 bitcast_convert_fusion
  52.0 2.1 %copy.268 = f32[8,128,128]{2,0,1:T(8,128)} copy(f32[8,128,128]{1,2,0:T(8,128)} %get-tuple-element.63) | data formatting | bytes 1048576
  54.1 1.9 multiply_reduce_fusion
  62.0 1.0 fusion.52
  68.2 1.0 fusion.101
  70.4 1.3 collective-permute-start.7
  71.9 1.3 collective-permute-start.8
  73.3 1.3 collective-permute-start.9
  74.6 1.3 collective-permute-start.10
  75.9 1.3 collective-permute-start.11
  78.2 1.3 collective-permute-start.12
  79.5 1.3 collective-permute-start.13
  83.2 2.7 %collective-permute-done.11 = bf16[128,256]{0,1:T(8,128)(2,1)S(1)} collective-permute-done((bf16[128,256]{0,1:T(8,128)(2,1)S(1)}, bf16[128,256]{0,1:T(8,128)(2,1)S(1)}, u32[]{:S(2)}, u32[]{:S(2)}) %collective-permute-start.11) | collective-permute-done | bytes 65568 | tf_op jit(solution)/shard_map/ppermute | solution.py:17
  86.0 4.8 %collective-permute-done.12 = bf16[128,256]{0,1:T(8,128)(2,1)S(1)} collective-permute-done((bf16[128,256]{0,1:T(8,128)(2,1)S(1)}, bf16[128,256]{0,1:T(8,128)(2,1)S(1)}, u32[]{:S(2)}, u32[]{:S(2)}) %collective-permute-start.12) | collective-permute-done | bytes 65568 | tf_op jit(solution)/shard_map/ppermute | solution.py:17
  90.8 2.4 %collective-permute-done.13 = bf16[128,256]{0,1:T(8,128)(2,1)S(1)} collective-permute-done((bf16[128,256]{0,1:T(8,128)(2,1)S(1)}, bf16[128,256]{0,1:T(8,128)(2,1)S(1)}, u32[]{:S(2)}, u32[]{:S(2)}) %collective-permute-start.13) | collective-permute-done | bytes 65568 | tf_op jit(solution)/shard_map/ppermute | solution.py:17
  93.4 113.7 %all-reduce = (f32[1024]{0:T(1024)S(1)}, f32[128]{0:T(128)S(1)}) all-reduce(f32[1024]{0:T(1024)S(1)} %bitcast.424, f32[128]{0:T(128)S(1)} %get-tuple-element.34), channel_id=1, replica_groups=mesh['seq'=64,'rep'=8] {'seq','rep'}, use_global_device_ids=true, to_apply=%region_26.27 | all-reduce | flops 1152 | bytes 9216 | tf_op jit(solution)/shard_map/psum | solution.py:130
  (168 shorter events, 34.2 us)
Async XLA Ops:
  0.6 22.6 %copy-start.8 = (bf16[1,128,1024]{2,1,0:T(8,128)(2,1)S(1)}, bf16[1,128,1024]{2,1,0:T(8,128)(2,1)}, u32[]{:S(2)}) copy-start(bf16[1,128,1024]{2,1,0:T(8,128)(2,1)} %param.7) | copy-start | bytes 786436
  2.1 22.6 %copy-start.10 = (bf16[1,128,256]{2,1,0:T(8,128)(2,1)}, bf16[1,128,256]{2,1,0:T(8,128)(2,1)S(1)}, u32[]{:S(2)}) copy-start(bf16[1,128,256]{2,1,0:T(8,128)(2,1)S(1)} %get-tuple-element.37) | copy-start | bytes 196612
  2.1 24.8 %collective-permute-start = (bf16[128,256]{1,0:T(8,128)(2,1)}, bf16[128,256]{1,0:T(8,128)(2,1)S(1)}, u32[]{:S(2)}, u32[]{:S(2)}) collective-permute-start(bf16[128,256]{1,0:T(8,128)(2,1)} %get-tuple-element.38), channel_id=1, source_target_pairs={{0,8},{8,16},{16,24},{24,32},{32,40},{40,48},{48,56},{56,64},{64,7... | collective-permute-start | bytes 196616 | tf_op jit(solution)/shard_map/ppermute | solution.py:17
  6.2 28.0 %collective-permute-start.2 = (bf16[128,256]{1,0:T(8,128)(2,1)}, bf16[128,256]{1,0:T(8,128)(2,1)S(1)}, u32[]{:S(2)}, u32[]{:S(2)}) collective-permute-start(bf16[128,256]{1,0:T(8,128)(2,1)} %get-tuple-element.38), channel_id=1, source_target_pairs={{0,24},{8,32},{16,40},{24,48},{32,56},{40,64},{48,72},{56,80},{64,... | collective-permute-start | bytes 196616 | tf_op jit(solution)/shard_map/ppermute | solution.py:17
  10.8 29.7 %collective-permute-start.3 = (bf16[128,256]{1,0:T(8,128)(2,1)}, bf16[128,256]{1,0:T(8,128)(2,1)S(1)}, u32[]{:S(2)}, u32[]{:S(2)}) collective-permute-start(bf16[128,256]{1,0:T(8,128)(2,1)} %get-tuple-element.38), channel_id=1, source_target_pairs={{0,32},{8,40},{16,48},{24,56},{32,64},{40,72},{48,80},{56,88},{64,... | collective-permute-start | bytes 196616 | tf_op jit(solution)/shard_map/ppermute | solution.py:17
  14.4 26.9 %collective-permute-start.1 = (bf16[128,256]{1,0:T(8,128)(2,1)}, bf16[128,256]{1,0:T(8,128)(2,1)S(1)}, u32[]{:S(2)}, u32[]{:S(2)}) collective-permute-start(bf16[128,256]{1,0:T(8,128)(2,1)} %get-tuple-element.38), channel_id=1, source_target_pairs={{0,16},{8,24},{16,32},{24,40},{32,48},{40,56},{48,64},{56,72},{64,... | collective-permute-start | bytes 196616 | tf_op jit(solution)/shard_map/ppermute | solution.py:17
  18.0 25.0 %collective-permute-start.4 = (bf16[128,256]{1,0:T(8,128)(2,1)}, bf16[128,256]{1,0:T(8,128)(2,1)}, u32[]{:S(2)}, u32[]{:S(2)}) collective-permute-start(bf16[128,256]{1,0:T(8,128)(2,1)} %get-tuple-element.38), channel_id=1, source_target_pairs={{0,40},{8,48},{16,56},{24,64},{32,72},{40,80},{48,88},{56,96},{64,... | collective-permute-start | bytes 196616 | tf_op jit(solution)/shard_map/ppermute | solution.py:17
  26.9 7.1 %copy-start.27 = (bf16[128,256]{1,0:T(8,128)(2,1)}, bf16[128,256]{1,0:T(8,128)(2,1)S(1)}, u32[]{:S(2)}) copy-start(bf16[128,256]{1,0:T(8,128)(2,1)S(1)} %collective-permute-done) | copy-start | bytes 196612
  26.9 17.2 %collective-permute-start.5 = (bf16[128,256]{1,0:T(8,128)(2,1)}, bf16[128,256]{1,0:T(8,128)(2,1)S(1)}, u32[]{:S(2)}, u32[]{:S(2)}) collective-permute-start(bf16[128,256]{1,0:T(8,128)(2,1)} %get-tuple-element.38), channel_id=1, source_target_pairs={{0,48},{8,56},{16,64},{24,72},{32,80},{40,88},{48,96},{56,104},{64... | collective-permute-start | bytes 196616 | tf_op jit(solution)/shard_map/ppermute | solution.py:17
  34.1 6.3 %copy-start.20 = (bf16[128,256]{1,0:T(8,128)(2,1)}, bf16[128,256]{1,0:T(8,128)(2,1)S(1)}, u32[]{:S(2)}) copy-start(bf16[128,256]{1,0:T(8,128)(2,1)S(1)} %collective-permute-done.2) | copy-start | bytes 196612
  34.1 10.4 %collective-permute-start.6 = (bf16[128,256]{1,0:T(8,128)(2,1)}, bf16[128,256]{1,0:T(8,128)(2,1)S(1)}, u32[]{:S(2)}, u32[]{:S(2)}) collective-permute-start(bf16[128,256]{1,0:T(8,128)(2,1)} %get-tuple-element.38), channel_id=1, source_target_pairs={{0,56},{8,64},{16,72},{24,80},{32,88},{40,96},{48,104},{56,112},{6... | collective-permute-start | bytes 196616 | tf_op jit(solution)/shard_map/ppermute | solution.py:17
  44.0 3.8 %copy-start = (f32[8,128,128]{1,2,0:T(8,128)}, f32[8,128,128]{1,2,0:T(8,128)S(1)}, u32[]{:S(2)}) copy-start(f32[8,128,128]{1,2,0:T(8,128)S(1)} %get-tuple-element.54) | copy-start | bytes 1572868
  44.1 4.7 %copy-start.23 = (bf16[128,256]{1,0:T(8,128)(2,1)}, bf16[128,256]{1,0:T(8,128)(2,1)S(1)}, u32[]{:S(2)}) copy-start(bf16[128,256]{1,0:T(8,128)(2,1)S(1)} %collective-permute-done.5) | copy-start | bytes 196612
  44.4 4.4 %copy-start.2 = (f32[8,128,128]{1,2,0:T(8,128)}, f32[8,128,128]{1,2,0:T(8,128)S(1)}, u32[]{:S(2)}) copy-start(f32[8,128,128]{1,2,0:T(8,128)S(1)} %get-tuple-element.52) | copy-start | bytes 1572868
  44.5 4.5 %copy-start.25 = (bf16[128,256]{1,0:T(8,128)(2,1)}, bf16[128,256]{1,0:T(8,128)(2,1)S(1)}, u32[]{:S(2)}) copy-start(bf16[128,256]{1,0:T(8,128)(2,1)S(1)} %collective-permute-done.6) | copy-start | bytes 196612
  44.8 4.3 %copy-start.4 = (f32[8,128,128]{1,2,0:T(8,128)}, f32[8,128,128]{1,2,0:T(8,128)S(1)}, u32[]{:S(2)}) copy-start(f32[8,128,128]{1,2,0:T(8,128)S(1)} %get-tuple-element.48) | copy-start | bytes 1572868
  52.0 2.1 %copy-start.7 = (bf16[16,8,8,128]{3,2,1,0:T(8,128)(2,1)S(1)}, bf16[16,8,8,128]{3,2,1,0:T(8,128)(2,1)}, u32[]{:S(2)}) copy-start(bf16[16,8,8,128]{3,2,1,0:T(8,128)(2,1)} %copy-done.6) | copy-start | bytes 786436
  70.4 7.8 %collective-permute-start.7 = (bf16[128,256]{0,1:T(8,128)(2,1)S(1)}, bf16[128,256]{0,1:T(8,128)(2,1)S(1)}, u32[]{:S(2)}, u32[]{:S(2)}) collective-permute-start(bf16[128,256]{0,1:T(8,128)(2,1)S(1)} %pad_maximum_fusion.1), channel_id=1, source_target_pairs={{8,0},{16,8},{24,16},{32,24},{40,32},{48,40},{56,48},{64,56},{72,6... | collective-permute-start | bytes 196616 | tf_op jit(solution)/shard_map/ppermute | solution.py:17
  71.9 7.5 %collective-permute-start.8 = (bf16[128,256]{0,1:T(8,128)(2,1)S(1)}, bf16[128,256]{0,1:T(8,128)(2,1)S(1)}, u32[]{:S(2)}, u32[]{:S(2)}) collective-permute-start(bf16[128,256]{0,1:T(8,128)(2,1)S(1)} %pad_maximum_fusion.2), channel_id=1, source_target_pairs={{16,0},{24,8},{32,16},{40,24},{48,32},{56,40},{64,48},{72,56},{80,... | collective-permute-start | bytes 196616 | tf_op jit(solution)/shard_map/ppermute | solution.py:17
  73.3 9.6 %collective-permute-start.9 = (bf16[128,256]{0,1:T(8,128)(2,1)S(1)}, bf16[128,256]{0,1:T(8,128)(2,1)S(1)}, u32[]{:S(2)}, u32[]{:S(2)}) collective-permute-start(bf16[128,256]{0,1:T(8,128)(2,1)S(1)} %pad_maximum_fusion.3), channel_id=1, source_target_pairs={{24,0},{32,8},{40,16},{48,24},{56,32},{64,40},{72,48},{80,56},{88,... | collective-permute-start | bytes 196616 | tf_op jit(solution)/shard_map/ppermute | solution.py:17
  74.6 8.7 %collective-permute-start.10 = (bf16[128,256]{0,1:T(8,128)(2,1)S(1)}, bf16[128,256]{0,1:T(8,128)(2,1)S(1)}, u32[]{:S(2)}, u32[]{:S(2)}) collective-permute-start(bf16[128,256]{0,1:T(8,128)(2,1)S(1)} %pad_maximum_fusion.4), channel_id=1, source_target_pairs={{32,0},{40,8},{48,16},{56,24},{64,32},{72,40},{80,48},{88,56},{96,... | collective-permute-start | bytes 196616 | tf_op jit(solution)/shard_map/ppermute | solution.py:17
  75.9 10.1 %collective-permute-start.11 = (bf16[128,256]{0,1:T(8,128)(2,1)S(1)}, bf16[128,256]{0,1:T(8,128)(2,1)S(1)}, u32[]{:S(2)}, u32[]{:S(2)}) collective-permute-start(bf16[128,256]{0,1:T(8,128)(2,1)S(1)} %pad_maximum_fusion.5), channel_id=1, source_target_pairs={{40,0},{48,8},{56,16},{64,24},{72,32},{80,40},{88,48},{96,56},{104... | collective-permute-start | bytes 196616 | tf_op jit(solution)/shard_map/ppermute | solution.py:17
  78.2 12.6 %collective-permute-start.12 = (bf16[128,256]{0,1:T(8,128)(2,1)S(1)}, bf16[128,256]{0,1:T(8,128)(2,1)S(1)}, u32[]{:S(2)}, u32[]{:S(2)}) collective-permute-start(bf16[128,256]{0,1:T(8,128)(2,1)S(1)} %pad_maximum_fusion.6), channel_id=1, source_target_pairs={{48,0},{56,8},{64,16},{72,24},{80,32},{88,40},{96,48},{104,56},{11... | collective-permute-start | bytes 196616 | tf_op jit(solution)/shard_map/ppermute | solution.py:17
  79.5 13.7 %collective-permute-start.13 = (bf16[128,256]{0,1:T(8,128)(2,1)S(1)}, bf16[128,256]{0,1:T(8,128)(2,1)S(1)}, u32[]{:S(2)}, u32[]{:S(2)}) collective-permute-start(bf16[128,256]{0,1:T(8,128)(2,1)S(1)} %pad_maximum_fusion.7), channel_id=1, source_target_pairs={{56,0},{64,8},{72,16},{80,24},{88,32},{96,40},{104,48},{112,56},{1... | collective-permute-start | bytes 196616 | tf_op jit(solution)/shard_map/ppermute | solution.py:17
  (23 other events, 19.8 us)
where the time goes:
time: 211 us; the launch traced here: 210 us
  blocking collectives  114 us (54%)
  starting transfers between devices  42 us (20%)
  local copies, waits for them, and re-layouts  18.8 us (9%)
  matrix products  16.5 us (8%)
  waiting for transfers between devices  10.4 us (5%)
  other arithmetic  6.65 us (3%)
    psum x1, blocking collectives, per_device(): q_total, v_total = lax.psum((q_sum, v_sum), ('seq', 'rep'))  114 us
    ppermute x14, starting transfers between devices, passed_along(): return lax.ppermute(block, axis, route)  42 us
    unnamed x73, local copies, waits for them, and re-layouts  17.5 us
    ppermute x14, waiting for transfers between devices, passed_along(): return lax.ppermute(block, axis, route)  10.4 us
  transfers between devices with their start and end apart: 14, of which 4 were waited for; matrix products, arithmetic and copies ran while one was open for 4% of the time, Pallas kernels for 0%

commit v1 on v0

v1 whole, which is shorter than its diff:
```python
import functools
import math

import jax
import jax.numpy as jnp
from jax import lax
from jax.experimental import pallas as pl
from jax.experimental.pallas import tpu as pltpu
from jax.sharding import Mesh
from jax.sharding import PartitionSpec as P

SPAN = 8
HEAD_GROUP = 2
masked_fill = -1e30
f32 = jnp.float32
bf16 = jnp.bfloat16


def transposed_product(a, b):
    return lax.dot_general(a, b, (((1,), (1,)), ((), ())), preferred_element_type=f32)


def attention_kernel(
    place, lengths, queries, out_grad, window, q_bias, v_bias,
    attended, q_grad, partials, q_sum, v_sum,
    value_rows, value_cols, key_cols, fill, key_acc, value_acc,
):
    tokens, head_dim = queries.shape[0], v_bias.shape[1]
    heads = queries.shape[1] // head_dim
    span = window.shape[0]
    reach = span * tokens
    scale = 1.0 / math.sqrt(head_dim)
    shard, member = place[0], place[1]

    query_pos = shard * tokens + lax.broadcasted_iota(jnp.int32, (1, tokens), 1)
    first = jnp.zeros((1, tokens), jnp.int32)
    end = jnp.int32(0)
    for doc in range(lengths.shape[1]):
        end = end + lengths[0, doc]
        first = jnp.where(end <= query_pos, end, first)

    for slot in range(span):
        rows = pl.ds(slot * tokens, tokens)
        owner = shard - member + slot - jnp.where(slot > member, span, 0)
        key_pos = owner * tokens + lax.broadcasted_iota(jnp.int32, (tokens, tokens), 0)
        allowed = (key_pos >= first) & (key_pos <= query_pos)
        fill[rows, :] = jnp.where(allowed, 0.0, masked_fill)
        values = (window[slot, :, head_dim:].astype(f32) + v_bias[...]).astype(bf16)
        value_rows[rows, :] = values
        value_cols[:, rows] = values.T
        key_cols[:, rows] = window[slot, :, :head_dim].T

    keys = window[:, :, :head_dim].reshape(reach, head_dim)
    fill_pair = jnp.concatenate([fill[...]] * HEAD_GROUP, axis=1)
    for first_head in range(0, heads, HEAD_GROUP):
        cols = [pl.ds((first_head + n) * head_dim, head_dim) for n in range(HEAD_GROUP)]
        query_rows = jnp.concatenate(
            [(queries[:, c].astype(f32) + q_bias[:, c]).astype(bf16) for c in cols], axis=0
        )
        grad_rows = jnp.concatenate([out_grad[:, c] for c in cols], axis=0)
        scores = transposed_product(keys, query_rows) * (scale * math.log2(math.e)) + fill_pair
        top = jnp.max(scores, axis=0, keepdims=True)
        powers = jnp.exp2(scores - top)
        weights = powers * (1.0 / jnp.sum(powers, axis=0, keepdims=True))
        probs = weights.astype(bf16)
        found = jnp.dot(value_cols[...], probs, preferred_element_type=f32).astype(bf16)
        grad_cols = grad_rows.T
        delta = jnp.sum(grad_cols.astype(f32) * found.astype(f32), axis=0, keepdims=True)
        d_probs = transposed_product(value_rows[...], grad_rows)
        d_scores = (weights * (d_probs - delta)).astype(bf16)
        q_part = jnp.dot(key_cols[...], d_scores, preferred_element_type=f32).T * scale
        found_rows = found.T
        for n, c in enumerate(cols):
            rows = slice(n * tokens, (n + 1) * tokens)
            attended[:, c] = found_rows[rows]
            q_grad[:, c] = q_part[rows]
            q_sum[:, c] = jnp.sum(q_part[rows], axis=0, keepdims=True)
        key_term = jnp.dot(d_scores, query_rows, preferred_element_type=f32)
        value_term = jnp.dot(probs, grad_rows, preferred_element_type=f32)
        if first_head == 0:
            key_acc[...] = key_term
            value_acc[...] = value_term
        else:
            key_acc[...] += key_term
            value_acc[...] += value_term
    partials[:, :, :head_dim] = (key_acc[...] * scale).astype(bf16).reshape(span, tokens, head_dim)
    partials[:, :, head_dim:] = value_acc[...].astype(bf16).reshape(span, tokens, head_dim)
    v_sum[...] = jnp.sum(value_acc[...], axis=0, keepdims=True)


def attention(place, lengths, queries, out_grad, window, q_bias, v_bias):
    tokens, width = queries.shape
    span, _, pair = window.shape
    head_dim = pair // 2
    reach = span * tokens
    vmem = pl.BlockSpec(memory_space=pltpu.VMEM)
    smem = pl.BlockSpec(memory_space=pltpu.SMEM)
    return pl.pallas_call(
        attention_kernel,
        out_shape=(
            jax.ShapeDtypeStruct((tokens, width), bf16),
            jax.ShapeDtypeStruct((tokens, width), f32),
            jax.ShapeDtypeStruct((span, tokens, pair), bf16),
            jax.ShapeDtypeStruct((1, width), f32),
            jax.ShapeDtypeStruct((1, head_dim), f32),
        ),
        in_specs=[smem, smem] + [vmem] * 5,
        out_specs=(vmem,) * 5,
        scratch_shapes=[
            pltpu.VMEM((reach, head_dim), bf16),
            pltpu.VMEM((head_dim, reach), bf16),
            pltpu.VMEM((head_dim, reach), bf16),
            pltpu.VMEM((reach, tokens), f32),
            pltpu.VMEM((reach, head_dim), f32),
            pltpu.VMEM((reach, head_dim), f32),
        ],
        compiler_params=pltpu.CompilerParams(vmem_limit_bytes=40 * 1024 * 1024),
        cost_estimate=pl.CostEstimate(
            flops=12 * width * reach * tokens,
            bytes_accessed=4 * tokens * width * 2,
            transcendentals=reach * width,
        ),
        name="attention",
    )(place, lengths, queries, out_grad, window, q_bias, v_bias)


def exchanged(blocks, axis):
    return lax.all_to_all(blocks, axis, 0, 0)


def summed_over(row, axis):
    size = lax.axis_size(axis)
    copies = jnp.broadcast_to(row[None], (size,) + row.shape)
    return jnp.sum(exchanged(copies, axis), axis=0)


def per_device(queries, keys, values, out_grad, q_bias, v_bias, doc_lengths):
    tokens, head_dim = keys.shape[1], keys.shape[2]
    width = queries.shape[2]
    groups, span = lax.axis_size("group"), lax.axis_size("member")
    group, member = lax.axis_index("group"), lax.axis_index("member")
    place = jnp.stack([group * span + member, member]).astype(jnp.int32)

    own = jnp.concatenate([keys[0], values[0]], axis=1)
    before = lax.ppermute(own, "group", [(i, i + 1) for i in range(groups - 1)])
    later = (jnp.arange(span) >= member)[:, None, None]
    window = exchanged(jnp.where(later, own[None], before[None]), "member")

    attended, q_grad, partials, q_sum, v_sum = attention(
        place, doc_lengths, queries[0], out_grad[0], window, q_bias[None], v_bias[None]
    )

    received = exchanged(partials, "member").astype(f32)
    mine = jnp.sum(jnp.where(later, received, 0.0), axis=0)
    others = jnp.sum(jnp.where(later, 0.0, received), axis=0)
    returned = lax.ppermute(others.astype(bf16), "group", [(i + 1, i) for i in range(groups - 1)])
    owned = mine + returned.astype(f32)

    sums = jnp.concatenate([q_sum[0], v_sum[0]])
    for axis in ("rep", "member", "group"):
        sums = summed_over(sums, axis)
    inverse = 1.0 / math.sqrt(groups * span * tokens * lax.axis_size("rep"))
    sums = sums * inverse
    return (
        attended[None],
        q_grad[None],
        owned[None, :, :head_dim],
        owned[None, :, head_dim:],
        sums[:width],
        sums[width:],
    )


def solution(mesh):
    fine = Mesh(
        mesh.devices.reshape(mesh.shape["seq"] // SPAN, SPAN, mesh.shape["rep"]),
        ("group", "member", "rep"),
    )
    tokens = P("rep", ("group", "member"), None)
    return jax.shard_map(
        per_device,
        mesh=fine,
        in_specs=(tokens, tokens, tokens, tokens, P(), P(), P("rep", None)),
        out_specs=(tokens, tokens, tokens, tokens, P(), P()),
        check_vma=False,
    )
```

time: 211 us -> 100 us (0.47)
  the two profiles are of different devices: /device:TPU:1 before, /device:TPU:2 now
where the time goes in v1:
time: 100 us; the launch traced here: 99.9 us
  blocking collectives  45.9 us (46%)
  waiting for transfers between devices  24.6 us (25%)
  starting transfers between devices  16.3 us (16%)
  Pallas kernels  7.79 us (8%)
  local copies, waits for them, and re-layouts  2.49 us (2%)
  other arithmetic  2.15 us (2%)
    all_to_all x3, blocking collectives, exchanged(): return lax.all_to_all(blocks, axis, 0, 0)  45.9 us
    all_to_all x2, waiting for transfers between devices, exchanged(): return lax.all_to_all(blocks, axis, 0, 0)  17.4 us
    all_to_all x2, starting transfers between devices, exchanged(): return lax.all_to_all(blocks, axis, 0, 0)  9.84 us
    pallas_call x1, Pallas kernels, attention(): pl.pallas_call(attention_kernel, out_shape=(jax.ShapeDtypeStruct((tokens,...  7.79 us
    ppermute x1, waiting for transfers between devices, per_device(): lax.ppermute(others.astype(bf16), 'group', [(i + 1, i) for i in range(gro...  5.24 us
    ppermute x1, starting transfers between devices, per_device(): before = lax.ppermute(own, 'group', [(i, i + 1) for i in range(groups - 1)])  5.17 us
  transfers between devices with their start and end apart: 4, of which 4 were waited for; matrix products, arithmetic and copies ran while one was open for 1% of the time, Pallas kernels for 0%

profile of v1, /device:TPU:2, one launch (start us, length us, event | category | flops | bytes accessed | tf_op | source)
XLA Modules:
  0.0 99.9 jit_solution(13006322390334567892)
XLA Ops:
  0.6 0.8 pad_maximum_fusion
  1.4 5.2 %collective-permute-start = (bf16[128,256]{1,0:T(8,128)(2,1)S(1)}, bf16[128,256]{1,0:T(8,128)(2,1)S(1)}, u32[]{:S(2)}, u32[]{:S(2)}) collective-permute-start(bf16[128,256]{1,0:T(8,128)(2,1)S(1)} %pad_maximum_fusion), channel_id=1, source_target_pairs={{0,64},{64,128},{128,192},{192,256},{256,320},{320,384},{384,448},... | collective-permute-start | bytes 196616 | tf_op jit(solution)/shard_map/ppermute | solution.py:145
  6.6 1.9 %collective-permute-done = bf16[128,256]{1,0:T(8,128)(2,1)S(1)} collective-permute-done((bf16[128,256]{1,0:T(8,128)(2,1)S(1)}, bf16[128,256]{1,0:T(8,128)(2,1)S(1)}, u32[]{:S(2)}, u32[]{:S(2)}) %collective-permute-start) | collective-permute-done | bytes 65568 | tf_op jit(solution)/shard_map/ppermute | solution.py:145
  8.5 0.9 broadcast_select_fusion
  9.4 6.4 %all-to-all-start = ((bf16[8,128,256]{2,1,0:T(8,128)(2,1)}), bf16[8,128,256]{2,1,0:T(8,128)(2,1)S(1)}, u32[]{:S(2)}, u32[]{:S(2)}) async-start(bf16[8,128,256]{2,1,0:T(8,128)(2,1)} %broadcast_select_fusion), calls=%async_computation | async-start | bytes 1048576 | tf_op jit(solution)/shard_map/all_to_all | solution.py:128
  15.7 0.1 pad_add_fusion.place
  15.8 9.3 %all-to-all-done.window = bf16[8,128,256]{2,1,0:T(8,128)(2,1)S(1)} async-done(((bf16[8,128,256]{2,1,0:T(8,128)(2,1)}), bf16[8,128,256]{2,1,0:T(8,128)(2,1)S(1)}, u32[]{:S(2)}, u32[]{:S(2)}) %all-to-all-start) | async-done | bytes 524320 | tf_op jit(solution)/shard_map/all_to_all | solution.py:128
  25.1 0.0 copy-done
  25.1 0.0 copy-done.1
  25.1 0.0 copy-done.2
  25.1 0.6 copy-done.3
  25.8 0.0 copy-done.4
  25.8 7.8 %attention.1 = (bf16[128,1024]{1,0:T(8,128)(2,1)}, f32[128,1024]{1,0:T(8,128)}, bf16[8,128,256]{2,1,0:T(8,128)(2,1)}, f32[1,1024]{1,0:T(1,128)S(1)}, f32[1,128]{1,0:T(1,128)S(1)}) custom-call(s32[2]{0:T(128)S(1)} %pad_add_fusion.place, s32[1,16]{1,0:T(1,128)S(1)} %copy-done.3, bf16[128,1024]{1,0:T(8,128)(2,1)S(1)} %bitcast.18, ...), custom_call_target="tpu_custom_call" | custom-call | flops 1610612736 | bytes 1048576 | tf_op jit(solution)/shard_map/attention/pallas_call | solution.py:98
  33.6 8.6 %all_to_all.28 = f32[8,1,1152]{2,1,0:T(1,128)S(1)} all-to-all(f32[8,1,1152]{2,1,0:T(1,128)S(1)} %broadcast_in_dim.91), channel_id=1, replica_groups=mesh['group'=8,'member'=8,'rep'=8] {'rep'}, dimensions={0} | all-to-all | bytes 73728 | tf_op jit(solution)/shard_map/all_to_all | solution.py:128
  42.3 9.2 %all_to_all.29 = f32[8,1,1152]{2,1,0:T(1,128)S(1)} all-to-all(f32[8,1,1152]{2,1,0:T(1,128)S(1)} %broadcast_in_dim.92), channel_id=1, replica_groups=mesh['group'=8,'member'=8,'rep'=8] {'member'}, dimensions={0} | all-to-all | bytes 73728 | tf_op jit(solution)/shard_map/all_to_all | solution.py:128
  51.6 28.0 %all_to_all.30 = f32[8,1,1152]{2,1,0:T(1,128)S(1)} all-to-all(f32[8,1,1152]{2,1,0:T(1,128)S(1)} %broadcast_in_dim.93), channel_id=1, replica_groups=mesh['group'=8,'member'=8,'rep'=8] {'group'}, dimensions={0} | all-to-all | bytes 73728 | tf_op jit(solution)/shard_map/all_to_all | solution.py:128
  79.6 3.5 %all-to-all-start.1 = ((bf16[8,128,256]{2,1,0:T(8,128)(2,1)}), bf16[8,128,256]{2,1,0:T(8,128)(2,1)S(1)}, u32[]{:S(2)}, u32[]{:S(2)}) async-start(bf16[8,128,256]{2,1,0:T(8,128)(2,1)} %get-tuple-element.13), calls=%async_computation.1 | async-start | bytes 1048576 | tf_op jit(solution)/shard_map/all_to_all | solution.py:128
  83.1 8.2 %all-to-all-done.1 = bf16[8,128,256]{2,1,0:T(8,128)(2,1)S(1)} async-done(((bf16[8,128,256]{2,1,0:T(8,128)(2,1)}), bf16[8,128,256]{2,1,0:T(8,128)(2,1)S(1)}, u32[]{:S(2)}, u32[]{:S(2)}) %all-to-all-start.1) | async-done | bytes 524320 | tf_op jit(solution)/shard_map/all_to_all | solution.py:128
  91.3 0.3 fusion.1
  91.6 1.3 %collective-permute-start.1 = (bf16[128,256]{1,0:T(8,128)(2,1)S(1)}, bf16[128,256]{1,0:T(8,128)(2,1)S(1)}, u32[]{:S(2)}, u32[]{:S(2)}) collective-permute-start(bf16[128,256]{1,0:T(8,128)(2,1)S(1)} %get-tuple-element.16), channel_id=1, source_target_pairs={{64,0},{128,64},{192,128},{256,192},{320,256},{384,320},{448,384},... | collective-permute-start | bytes 196616 | tf_op jit(solution)/shard_map/ppermute | solution.py:156
  92.9 0.6 slice.18
  93.5 0.5 slice.19
  94.0 5.2 %collective-permute-done.1 = bf16[128,256]{1,0:T(8,128)(2,1)S(1)} collective-permute-done((bf16[128,256]{1,0:T(8,128)(2,1)S(1)}, bf16[128,256]{1,0:T(8,128)(2,1)S(1)}, u32[]{:S(2)}, u32[]{:S(2)}) %collective-permute-start.1) | collective-permute-done | bytes 65568 | tf_op jit(solution)/shard_map/ppermute | solution.py:156
  99.3 0.7 slice_bitcast_fusion
  (15 shorter events, 0.2 us)
Async XLA Ops:
  1.4 7.1 %collective-permute-start = (bf16[128,256]{1,0:T(8,128)(2,1)S(1)}, bf16[128,256]{1,0:T(8,128)(2,1)S(1)}, u32[]{:S(2)}, u32[]{:S(2)}) collective-permute-start(bf16[128,256]{1,0:T(8,128)(2,1)S(1)} %pad_maximum_fusion), channel_id=1, source_target_pairs={{0,64},{64,128},{128,192},{192,256},{256,320},{320,384},{384,448},... | collective-permute-start | bytes 196616 | tf_op jit(solution)/shard_map/ppermute | solution.py:145
  9.4 15.7 %copy-start = (bf16[1,128,1024]{2,1,0:T(8,128)(2,1)S(1)}, bf16[1,128,1024]{2,1,0:T(8,128)(2,1)}, u32[]{:S(2)}) copy-start(bf16[1,128,1024]{2,1,0:T(8,128)(2,1)} %param.7) | copy-start | bytes 786436
  9.4 15.7 %copy-start.1 = (bf16[1,128,1024]{2,1,0:T(8,128)(2,1)S(1)}, bf16[1,128,1024]{2,1,0:T(8,128)(2,1)}, u32[]{:S(2)}) copy-start(bf16[1,128,1024]{2,1,0:T(8,128)(2,1)} %param.10) | copy-start | bytes 786436
  9.4 15.7 %all-to-all-start = ((bf16[8,128,256]{2,1,0:T(8,128)(2,1)}), bf16[8,128,256]{2,1,0:T(8,128)(2,1)S(1)}, u32[]{:S(2)}, u32[]{:S(2)}) async-start(bf16[8,128,256]{2,1,0:T(8,128)(2,1)} %broadcast_select_fusion), calls=%async_computation | async-start | bytes 1048576 | tf_op jit(solution)/shard_map/all_to_all | solution.py:128
  15.8 9.3 %copy-start.2 = (f32[1024]{0:T(1024)S(1)}, f32[1024]{0:T(1024)}, u32[]{:S(2)}) copy-start(f32[1024]{0:T(1024)} %param.11) | copy-start | bytes 12292
  25.1 0.7 copy-start.3
  25.1 0.7 copy-start.4
  79.6 11.7 %all-to-all-start.1 = ((bf16[8,128,256]{2,1,0:T(8,128)(2,1)}), bf16[8,128,256]{2,1,0:T(8,128)(2,1)S(1)}, u32[]{:S(2)}, u32[]{:S(2)}) async-start(bf16[8,128,256]{2,1,0:T(8,128)(2,1)} %get-tuple-element.13), calls=%async_computation.1 | async-start | bytes 1048576 | tf_op jit(solution)/shard_map/all_to_all | solution.py:128
  91.6 7.7 %collective-permute-start.1 = (bf16[128,256]{1,0:T(8,128)(2,1)S(1)}, bf16[128,256]{1,0:T(8,128)(2,1)S(1)}, u32[]{:S(2)}, u32[]{:S(2)}) collective-permute-start(bf16[128,256]{1,0:T(8,128)(2,1)S(1)} %get-tuple-element.16), channel_id=1, source_target_pairs={{64,0},{128,64},{192,128},{256,192},{320,256},{384,320},{448,384},... | collective-permute-start | bytes 196616 | tf_op jit(solution)/shard_map/ppermute | solution.py:156

commit v2 on v1

v2 whole, which is shorter than its diff:
```python
import functools
import math

import jax
import jax.numpy as jnp
from jax import lax
from jax.experimental import pallas as pl
from jax.experimental.pallas import tpu as pltpu
from jax.sharding import Mesh
from jax.sharding import PartitionSpec as P

SPAN = 8
HEAD_GROUP = 2
SUM_ROWS = 16
masked_fill = -1e30
f32 = jnp.float32
bf16 = jnp.bfloat16


def transposed_product(a, b):
    return lax.dot_general(a, b, (((1,), (1,)), ((), ())), preferred_element_type=f32)


def attention_kernel(
    place, lengths, queries, out_grad, window, q_bias, v_bias,
    attended, q_grad, partials,
    value_rows, value_cols, key_cols, fill, key_acc, value_acc, sum_rows,
):
    step, last = pl.program_id(0), pl.num_programs(0) - 1
    span, _, pair = window.shape
    tokens, head_dim = queries.shape[0], pair // 2
    reach = span * tokens
    scale = 1.0 / math.sqrt(head_dim)
    shard, member = place[0], place[1]

    @pl.when(step == 0)
    def prepare():
        query_pos = shard * tokens + lax.broadcasted_iota(jnp.int32, (1, tokens), 1)
        first = jnp.zeros((1, tokens), jnp.int32)
        end = jnp.int32(0)
        for doc in range(lengths.shape[1]):
            end = end + lengths[0, doc]
            first = jnp.where(end <= query_pos, end, first)

        for slot in range(span):
            rows = pl.ds(slot * tokens, tokens)
            owner = shard - member + slot - jnp.where(slot > member, span, 0)
            key_pos = owner * tokens + lax.broadcasted_iota(jnp.int32, (tokens, tokens), 0)
            allowed = (key_pos >= first) & (key_pos <= query_pos)
            fill[rows, :] = jnp.where(allowed, 0.0, masked_fill)
            values = (window[slot, :, head_dim:].astype(f32) + v_bias[...]).astype(bf16)
            value_rows[rows, :] = values
            value_cols[:, rows] = values.T
            key_cols[:, rows] = window[slot, :, :head_dim].T
        key_acc[...] = jnp.zeros_like(key_acc)
        value_acc[...] = jnp.zeros_like(value_acc)
        sum_rows[...] = jnp.zeros_like(sum_rows)

    keys = window[:, :, :head_dim].reshape(reach, head_dim)
    halves = [slice(n * head_dim, (n + 1) * head_dim) for n in range(HEAD_GROUP)]
    query_rows = jnp.concatenate(
        [(queries[:, c].astype(f32) + q_bias[:, c]).astype(bf16) for c in halves], axis=0
    )
    grad_rows = jnp.concatenate([out_grad[:, c] for c in halves], axis=0)
    fill_pair = jnp.concatenate([fill[...]] * HEAD_GROUP, axis=1)
    scores = transposed_product(keys, query_rows) * (scale * math.log2(math.e)) + fill_pair
    top = jnp.max(scores, axis=0, keepdims=True)
    powers = jnp.exp2(scores - top)
    weights = powers * (1.0 / jnp.sum(powers, axis=0, keepdims=True))
    probs = weights.astype(bf16)
    found = jnp.dot(value_cols[...], probs, preferred_element_type=f32).astype(bf16)
    grad_cols = grad_rows.T
    delta = jnp.sum(grad_cols.astype(f32) * found.astype(f32), axis=0, keepdims=True)
    d_probs = transposed_product(value_rows[...], grad_rows)
    d_scores = (weights * (d_probs - delta)).astype(bf16)
    q_part = jnp.dot(key_cols[...], d_scores, preferred_element_type=f32).T * scale
    found_rows = found.T
    sums = []
    for n, c in enumerate(halves):
        rows = slice(n * tokens, (n + 1) * tokens)
        attended[:, c] = found_rows[rows]
        q_grad[:, c] = q_part[rows]
        sums.append(jnp.sum(q_part[rows], axis=0, keepdims=True))
    key_acc[...] += jnp.dot(d_scores, query_rows, preferred_element_type=f32)
    value_acc[...] += jnp.dot(probs, grad_rows, preferred_element_type=f32)

    def spread(row, value):
        high = value.astype(bf16)
        low = (value - high.astype(f32)).astype(bf16)
        sum_rows[pl.ds(row, 1), :] = high.astype(f32)
        sum_rows[pl.ds(row + SUM_ROWS // 2, 1), :] = low.astype(f32)

    spread(step, jnp.concatenate(sums, axis=1))

    @pl.when(step == last)
    def finish():
        value_sum = jnp.sum(value_acc[...], axis=0, keepdims=True)
        spread(last + 1, jnp.concatenate([value_sum, jnp.zeros_like(value_sum)], axis=1))
        parts = jnp.concatenate([key_acc[...] * scale, value_acc[...]], axis=1).astype(bf16)
        partials[:, :tokens, :] = parts.reshape(span, tokens, pair)
        partials[:, tokens:, :] = jnp.broadcast_to(
            sum_rows[...].astype(bf16)[None], (span, SUM_ROWS, pair)
        )


def attention(place, lengths, queries, out_grad, window, q_bias, v_bias):
    tokens, width = queries.shape
    span, _, pair = window.shape
    head_dim = pair // 2
    reach = span * tokens
    step_cols = HEAD_GROUP * head_dim
    smem = pl.BlockSpec(memory_space=pltpu.SMEM)
    head_cols = pl.BlockSpec((tokens, step_cols), lambda i: (0, i))

    def whole(*shape):
        return pl.BlockSpec(shape, lambda i: (0,) * len(shape))

    return pl.pallas_call(
        attention_kernel,
        grid=(width // step_cols,),
        out_shape=(
            jax.ShapeDtypeStruct((tokens, width), bf16),
            jax.ShapeDtypeStruct((tokens, width), f32),
            jax.ShapeDtypeStruct((span, tokens + SUM_ROWS, pair), bf16),
        ),
        in_specs=[
            smem,
            smem,
            head_cols,
            head_cols,
            whole(span, tokens, pair),
            pl.BlockSpec((1, step_cols), lambda i: (0, i)),
            whole(1, head_dim),
        ],
        out_specs=(head_cols, head_cols, whole(span, tokens + SUM_ROWS, pair)),
        scratch_shapes=[
            pltpu.VMEM((reach, head_dim), bf16),
            pltpu.VMEM((head_dim, reach), bf16),
            pltpu.VMEM((head_dim, reach), bf16),
            pltpu.VMEM((reach, tokens), f32),
            pltpu.VMEM((reach, head_dim), f32),
            pltpu.VMEM((reach, head_dim), f32),
            pltpu.VMEM((SUM_ROWS, pair), f32),
        ],
        compiler_params=pltpu.CompilerParams(vmem_limit_bytes=40 * 1024 * 1024),
        cost_estimate=pl.CostEstimate(
            flops=12 * width * reach * tokens,
            bytes_accessed=4 * tokens * width * 2,
            transcendentals=reach * width,
        ),
        name="attention",
    )(place, lengths, queries, out_grad, window, q_bias, v_bias)


def combine_kernel(place, received, mine, others, sums):
    span, rows, _ = received.shape
    tokens = rows - SUM_ROWS
    member = place[1]
    own = jnp.zeros(mine.shape, f32)
    other = jnp.zeros(mine.shape, f32)
    sum_rows = jnp.zeros((SUM_ROWS, received.shape[2]), f32)
    for slot in range(span):
        part = received[slot, :tokens, :].astype(f32)
        own += jnp.where(slot >= member, part, 0.0)
        other += jnp.where(slot >= member, 0.0, part)
        sum_rows += received[slot, tokens:, :].astype(f32)
    mine[...] = own
    others[...] = other.astype(bf16)
    whole_rows = sum_rows[: SUM_ROWS // 2] + sum_rows[SUM_ROWS // 2 :]
    pair = received.shape[2]
    for copy in range(sums.shape[0]):
        for start in range(0, sums.shape[2], pair):
            size = min(pair, sums.shape[2] - start)
            row = start // pair
            sums[copy, :, start : start + size] = whole_rows[row : row + 1, :size]


def combine(place, received, copies, width):
    span, rows, pair = received.shape
    vmem = pl.BlockSpec(memory_space=pltpu.VMEM)
    return pl.pallas_call(
        combine_kernel,
        out_shape=(
            jax.ShapeDtypeStruct((rows - SUM_ROWS, pair), f32),
            jax.ShapeDtypeStruct((rows - SUM_ROWS, pair), bf16),
            jax.ShapeDtypeStruct((copies, 1, width), f32),
        ),
        in_specs=[pl.BlockSpec(memory_space=pltpu.SMEM), vmem],
        out_specs=(vmem,) * 3,
        name="combine",
    )(place, received)


def exchanged(blocks, axis):
    return lax.all_to_all(blocks, axis, 0, 0)


def per_device(queries, keys, values, out_grad, q_bias, v_bias, doc_lengths):
    tokens, head_dim = keys.shape[1], keys.shape[2]
    width = queries.shape[2]
    groups, span = lax.axis_size("group"), lax.axis_size("member")
    group, member = lax.axis_index("group"), lax.axis_index("member")
    place = jnp.stack([group * span + member, member]).astype(jnp.int32)

    own = jnp.concatenate([keys[0], values[0]], axis=1)
    before = lax.ppermute(own, "group", [(i, i + 1) for i in range(groups - 1)])
    later = (jnp.arange(span) >= member)[:, None, None]
    window = exchanged(jnp.where(later, own[None], before[None]), "member")

    attended, q_grad, partials = attention(
        place, doc_lengths, queries[0], out_grad[0], window, q_bias[None], v_bias[None]
    )

    received = exchanged(partials, "member")
    mine, others, copies = combine(place, received, lax.axis_size("rep"), width + head_dim)
    returned = lax.ppermute(others, "group", [(i + 1, i) for i in range(groups - 1)])
    owned = mine + returned.astype(f32)

    rep_sums = jnp.sum(exchanged(copies, "rep"), axis=0)
    rep_sums, owned = lax.optimization_barrier((rep_sums, owned))
    copies = jnp.broadcast_to(rep_sums[None], (groups,) + rep_sums.shape)
    sums = jnp.sum(exchanged(copies, "group"), axis=(0, 1))
    inverse = 1.0 / math.sqrt(groups * span * tokens * lax.axis_size("rep"))
    sums = sums * inverse
    return (
        attended[None],
        q_grad[None],
        owned[None, :, :head_dim],
        owned[None, :, head_dim:],
        sums[:width],
        sums[width:],
    )


def solution(mesh):
    fine = Mesh(
        mesh.devices.reshape(mesh.shape["seq"] // SPAN, SPAN, mesh.shape["rep"]),
        ("group", "member", "rep"),
    )
    tokens = P("rep", ("group", "member"), None)
    return jax.shard_map(
        per_device,
        mesh=fine,
        in_specs=(tokens, tokens, tokens, tokens, P(), P(), P("rep", None)),
        out_specs=(tokens, tokens, tokens, tokens, P(), P()),
        check_vma=False,
    )
```

time: 100 us -> 90.8 us (0.908)
  the two profiles are of different devices: /device:TPU:2 before, /device:TPU:1 now
where the time goes in v2:
time: 90.8 us; the launch traced here: 90.3 us
  starting transfers between devices  28.2 us (31%)
  blocking collectives  26.1 us (29%)
  waiting for transfers between devices  19.8 us (22%)
  Pallas kernels  10.5 us (12%)
  local copies, waits for them, and re-layouts  3.05 us (3%)
  other arithmetic  1.87 us (2%)
    all_to_all x2, blocking collectives, exchanged(): return lax.all_to_all(blocks, axis, 0, 0)  26.1 us
    all_to_all x2, starting transfers between devices, exchanged(): return lax.all_to_all(blocks, axis, 0, 0)  21.1 us
    all_to_all x2, waiting for transfers between devices, exchanged(): return lax.all_to_all(blocks, axis, 0, 0)  18.5 us
    pallas_call x1, Pallas kernels, attention(): pl.pallas_call(attention_kernel, grid=(width // step_cols,), out_shape=(j...  8.57 us
    ppermute x1, starting transfers between devices, per_device(): before = lax.ppermute(own, 'group', [(i, i + 1) for i in range(groups - 1)])  5.72 us
    pallas_call x1, Pallas kernels, combine(): pl.pallas_call(combine_kernel, out_shape=(jax.ShapeDtypeStruct((rows - SU...  1.94 us
  transfers between devices with their start and end apart: 4, of which 3 were waited for; matrix products, arithmetic and copies ran while one was open for 1% of the time, Pallas kernels for 0%

profile of v2, /device:TPU:1, one launch (start us, length us, event | category | flops | bytes accessed | tf_op | source)
XLA Modules:
  0.0 90.3 jit_solution(8184236375618851861)
XLA Ops:
  0.6 0.8 pad_maximum_fusion
  1.4 5.7 %collective-permute-start = (bf16[128,256]{1,0:T(8,128)(2,1)S(1)}, bf16[128,256]{1,0:T(8,128)(2,1)S(1)}, u32[]{:S(2)}, u32[]{:S(2)}) collective-permute-start(bf16[128,256]{1,0:T(8,128)(2,1)S(1)} %pad_maximum_fusion), channel_id=1, source_target_pairs={{0,64},{64,128},{128,192},{192,256},{256,320},{320,384},{384,448},... | collective-permute-start | bytes 196616 | tf_op jit(solution)/shard_map/ppermute | solution.py:206
  7.2 1.3 %collective-permute-done = bf16[128,256]{1,0:T(8,128)(2,1)S(1)} collective-permute-done((bf16[128,256]{1,0:T(8,128)(2,1)S(1)}, bf16[128,256]{1,0:T(8,128)(2,1)S(1)}, u32[]{:S(2)}, u32[]{:S(2)}) %collective-permute-start) | collective-permute-done | bytes 65568 | tf_op jit(solution)/shard_map/ppermute | solution.py:206
  8.5 0.9 broadcast_select_fusion
  9.4 6.6 %all-to-all-start = ((bf16[8,128,256]{2,1,0:T(8,128)(2,1)}), bf16[8,128,256]{2,1,0:T(8,128)(2,1)S(1)}, u32[]{:S(2)}, u32[]{:S(2)}) async-start(bf16[8,128,256]{2,1,0:T(8,128)(2,1)} %broadcast_select_fusion), calls=%async_computation | async-start | bytes 1048576 | tf_op jit(solution)/shard_map/all_to_all | solution.py:195
  16.0 0.1 pad_add_fusion.place
  16.1 7.5 %all-to-all-done.window = bf16[8,128,256]{2,1,0:T(8,128)(2,1)S(1)} async-done(((bf16[8,128,256]{2,1,0:T(8,128)(2,1)}), bf16[8,128,256]{2,1,0:T(8,128)(2,1)S(1)}, u32[]{:S(2)}, u32[]{:S(2)}) %all-to-all-start) | async-done | bytes 524320 | tf_op jit(solution)/shard_map/all_to_all | solution.py:195
  23.5 0.0 copy-done
  23.5 0.0 copy-done.1
  23.5 0.0 copy-done.2
  23.5 0.6 copy-done.4
  24.2 0.0 copy-done.5
  24.2 8.6 %attention.1 = (bf16[128,1024]{1,0:T(8,128)(2,1)}, f32[128,1024]{1,0:T(8,128)}, bf16[8,144,256]{2,1,0:T(8,128)(2,1)S(1)}) custom-call(s32[2]{0:T(128)S(1)} %pad_add_fusion.place, s32[1,16]{1,0:T(1,128)S(1)} %copy-done.4, bf16[128,1024]{1,0:T(8,128)(2,1)S(1)} %bitcast.14, bf16[128,1024]{1,0:T(8,128)(2,1)S(1)} %bitcast.15, ...), custom_call_target="tpu_custom_call" | custom-call | flops 1610612736 | bytes 1048576 | tf_op jit(solution)/shard_map/attention/pallas_call | solution.py:118
  32.8 14.7 %all_to_all.20.received = bf16[8,144,256]{2,1,0:T(8,128)(2,1)} all-to-all(bf16[8,144,256]{2,1,0:T(8,128)(2,1)S(1)} %get-tuple-element.16), channel_id=1, replica_groups=mesh['group'=8,'member'=8,'rep'=8] {'member'}, dimensions={0} | all-to-all | bytes 1179648 | tf_op jit(solution)/shard_map/all_to_all | solution.py:195
  47.5 1.9 %combine.1 = (f32[128,256]{1,0:T(8,128)}, bf16[128,256]{1,0:T(8,128)(2,1)}, f32[8,1,1152]{2,1,0:T(1,128)}) custom-call(s32[2]{0:T(128)} %copy-done, bf16[8,144,256]{2,1,0:T(8,128)(2,1)} %all_to_all.20.received), custom_call_target="tpu_custom_call" | custom-call | tf_op jit(solution)/shard_map/combine/pallas_call | solution.py:181
  49.4 1.4 %collective-permute-start.1 = (bf16[128,256]{1,0:T(8,128)(2,1)}, bf16[128,256]{1,0:T(8,128)(2,1)S(1)}, u32[]{:S(2)}, u32[]{:S(2)}) collective-permute-start(bf16[128,256]{1,0:T(8,128)(2,1)} %get-tuple-element.19), channel_id=1, source_target_pairs={{64,0},{128,64},{192,128},{256,192},{320,256},{384,320},{448,384},... | collective-permute-start | bytes 196616 | tf_op jit(solution)/shard_map/ppermute | solution.py:216
  50.8 11.3 %all_to_all.21 = f32[8,1,1152]{2,1,0:T(1,128)S(1)} all-to-all(f32[8,1,1152]{2,1,0:T(1,128)} %get-tuple-element.17), channel_id=1, replica_groups=mesh['group'=8,'member'=8,'rep'=8] {'rep'}, dimensions={0} | all-to-all | bytes 73728 | tf_op jit(solution)/shard_map/all_to_all | solution.py:195
  62.2 0.0 collective-permute-done.1
  62.3 0.6 broadcast_in_dim.63
  62.9 14.4 %all-to-all-start.3 = ((f32[8,1,1152]{2,1,0:T(1,128)}), f32[8,1,1152]{2,1,0:T(1,128)S(1)}, u32[]{:S(2)}, u32[]{:S(2)}) async-start(f32[8,1,1152]{2,1,0:T(1,128)} %broadcast_in_dim.63), calls=%async_computation.3 | async-start | bytes 73728 | tf_op jit(solution)/shard_map/all_to_all | solution.py:195
  77.4 0.7 slice_bitcast_fusion
  78.0 11.1 %all-to-all-done.3 = f32[8,1,1152]{2,1,0:T(1,128)S(1)} async-done(((f32[8,1,1152]{2,1,0:T(1,128)}), f32[8,1,1152]{2,1,0:T(1,128)S(1)}, u32[]{:S(2)}, u32[]{:S(2)}) %all-to-all-start.3) | async-done | bytes 36896 | tf_op jit(solution)/shard_map/all_to_all | solution.py:195
  89.1 0.5 slice.17
  89.7 0.6 slice.16
  (16 shorter events, 0.1 us)
Async XLA Ops:
  1.4 7.0 %collective-permute-start = (bf16[128,256]{1,0:T(8,128)(2,1)S(1)}, bf16[128,256]{1,0:T(8,128)(2,1)S(1)}, u32[]{:S(2)}, u32[]{:S(2)}) collective-permute-start(bf16[128,256]{1,0:T(8,128)(2,1)S(1)} %pad_maximum_fusion), channel_id=1, source_target_pairs={{0,64},{64,128},{128,192},{192,256},{256,320},{320,384},{384,448},... | collective-permute-start | bytes 196616 | tf_op jit(solution)/shard_map/ppermute | solution.py:206
  9.4 14.2 %copy-start.1 = (bf16[1,128,1024]{2,1,0:T(8,128)(2,1)S(1)}, bf16[1,128,1024]{2,1,0:T(8,128)(2,1)}, u32[]{:S(2)}) copy-start(bf16[1,128,1024]{2,1,0:T(8,128)(2,1)} %param.7) | copy-start | bytes 786436
  9.4 14.2 %copy-start.2 = (bf16[1,128,1024]{2,1,0:T(8,128)(2,1)S(1)}, bf16[1,128,1024]{2,1,0:T(8,128)(2,1)}, u32[]{:S(2)}) copy-start(bf16[1,128,1024]{2,1,0:T(8,128)(2,1)} %param.10) | copy-start | bytes 786436
  9.4 14.1 %all-to-all-start = ((bf16[8,128,256]{2,1,0:T(8,128)(2,1)}), bf16[8,128,256]{2,1,0:T(8,128)(2,1)S(1)}, u32[]{:S(2)}, u32[]{:S(2)}) async-start(bf16[8,128,256]{2,1,0:T(8,128)(2,1)} %broadcast_select_fusion), calls=%async_computation | async-start | bytes 1048576 | tf_op jit(solution)/shard_map/all_to_all | solution.py:195
  16.1 7.5 %copy-start = (s32[2]{0:T(128)}, s32[2]{0:T(128)S(1)}, u32[]{:S(2)}) copy-start(s32[2]{0:T(128)S(1)} %pad_add_fusion.place) | copy-start | bytes 28
  16.1 7.5 %copy-start.3 = (f32[1024]{0:T(1024)S(1)}, f32[1024]{0:T(1024)}, u32[]{:S(2)}) copy-start(f32[1024]{0:T(1024)} %param.11) | copy-start | bytes 12292
  23.5 0.7 copy-start.4
  23.5 0.7 copy-start.5
  49.4 12.8 %copy-start.6 = (f32[128,256]{1,0:T(8,128)S(1)}, f32[128,256]{1,0:T(8,128)}, u32[]{:S(2)}) copy-start(f32[128,256]{1,0:T(8,128)} %get-tuple-element.18) | copy-start | bytes 393220
  49.4 12.8 %collective-permute-start.1 = (bf16[128,256]{1,0:T(8,128)(2,1)}, bf16[128,256]{1,0:T(8,128)(2,1)S(1)}, u32[]{:S(2)}, u32[]{:S(2)}) collective-permute-start(bf16[128,256]{1,0:T(8,128)(2,1)} %get-tuple-element.19), channel_id=1, source_target_pairs={{64,0},{128,64},{192,128},{256,192},{320,256},{384,320},{448,384},... | collective-permute-start | bytes 196616 | tf_op jit(solution)/shard_map/ppermute | solution.py:216
  62.9 26.2 %all-to-all-start.3 = ((f32[8,1,1152]{2,1,0:T(1,128)}), f32[8,1,1152]{2,1,0:T(1,128)S(1)}, u32[]{:S(2)}, u32[]{:S(2)}) async-start(f32[8,1,1152]{2,1,0:T(1,128)} %broadcast_in_dim.63), calls=%async_computation.3 | async-start | bytes 73728 | tf_op jit(solution)/shard_map/all_to_all | solution.py:195

commit v3 on v1

v3 whole, which is shorter than its diff:
```python
import functools
import math

import jax
import jax.numpy as jnp
from jax import lax
from jax.experimental import pallas as pl
from jax.experimental.pallas import tpu as pltpu
from jax.sharding import Mesh
from jax.sharding import PartitionSpec as P

SPAN = 8
HEAD_GROUP = 2
SEQ = ("z", "y")
MEMBER_FIRST = 0
LINE_FIRST = 5
SUM_ROWS = 16
masked_fill = -1e30
f32 = jnp.float32
bf16 = jnp.bfloat16


def transposed_product(a, b):
    return lax.dot_general(a, b, (((1,), (1,)), ((), ())), preferred_element_type=f32)


def attention_kernel(
    place, queries, out_grad, window, bias,
    attended, q_grad, partials,
    value_rows, key_cols, value_cols, fill, score, power, d_score, query_all, grad_all, sums,
):
    span, tokens, pair = window.shape
    head_dim = pair // 2
    width = queries.shape[1]
    reach = span * tokens
    both = HEAD_GROUP * tokens
    scale = 1.0 / math.sqrt(head_dim)
    shard, member = place[0], place[1]

    query_pos = shard * tokens + lax.broadcasted_iota(jnp.int32, (1, tokens), 1)
    first = jnp.zeros((1, tokens), jnp.int32)
    end = jnp.int32(0)
    for doc in range(2, place.shape[0]):
        end = end + place[doc]
        first = jnp.where(end <= query_pos, end, first)

    for slot in range(span):
        rows = pl.ds(slot * tokens, tokens)
        sender = (slot + MEMBER_FIRST) % span
        owner = shard - member + sender - jnp.where(sender > member, span, 0)
        key_pos = owner * tokens + lax.broadcasted_iota(jnp.int32, (tokens, tokens), 0)
        allowed = (key_pos >= first) & (key_pos <= query_pos)
        fill[rows, :] = jnp.where(allowed, 0.0, masked_fill)
        values = (window[slot, :, head_dim:].astype(f32) + bias[:, width:]).astype(bf16)
        value_rows[rows, :] = values
        value_cols[:, rows] = values.T
        key_cols[:, rows] = window[slot, :, :head_dim].T

    def scored(group):
        cols = [pl.ds((group * HEAD_GROUP + n) * head_dim, head_dim) for n in range(HEAD_GROUP)]
        query_rows = jnp.concatenate(
            [(queries[:, c].astype(f32) + bias[:, c]).astype(bf16) for c in cols], axis=0
        )
        grad_rows = jnp.concatenate([out_grad[:, c] for c in cols], axis=0)
        top = jnp.full((8, both), masked_fill, f32)
        for slot in range(span):
            rows = pl.ds(slot * tokens, tokens)
            part = transposed_product(window[slot, :, :head_dim], query_rows)
            part = part * (scale * math.log2(math.e)) + jnp.concatenate([fill[rows, :]] * 2, axis=1)
            score[group % 2, rows, :] = part
            top = jnp.maximum(top, jnp.max(part.reshape(tokens // 8, 8, both), axis=0))
        return query_rows, grad_rows, jnp.max(top, axis=0, keepdims=True)

    def finished(group, query_rows, grad_rows, top):
        here = pl.ds(group * both, both)
        total = jnp.zeros((8, both), f32)
        for slot in range(span):
            rows = pl.ds(slot * tokens, tokens)
            part = jnp.exp2(score[group % 2, rows, :] - top)
            total += jnp.sum(part.reshape(tokens // 8, 8, both), axis=0)
            power[rows, here] = part.astype(bf16)
        inverse = 1.0 / jnp.sum(total, axis=0, keepdims=True)
        found = jnp.dot(value_cols[...], power[:, here], preferred_element_type=f32) * inverse
        found = found.astype(bf16)
        grad_cols = grad_rows.T
        delta = jnp.sum(grad_cols.astype(f32) * found.astype(f32), axis=0, keepdims=True)
        for slot in range(span):
            rows = pl.ds(slot * tokens, tokens)
            d_probs = transposed_product(value_rows[rows, :], grad_rows)
            d_score[rows, here] = power[rows, here] * (d_probs - delta).astype(bf16)
        q_part = jnp.dot(key_cols[...], d_score[:, here], preferred_element_type=f32)
        q_part = (q_part * (inverse * scale)).T
        found = found.T
        column = jnp.broadcast_to(inverse, (head_dim, both)).T
        query_all[here, :] = (query_rows.astype(f32) * (column * scale)).astype(bf16)
        grad_all[here, :] = (grad_rows.astype(f32) * column).astype(bf16)
        for n in range(HEAD_GROUP):
            c = pl.ds((group * HEAD_GROUP + n) * head_dim, head_dim)
            rows = slice(n * tokens, (n + 1) * tokens)
            attended[:, c] = found[rows]
            q_grad[:, c] = q_part[rows]
            sums[group : group + 1, n * head_dim : (n + 1) * head_dim] = jnp.sum(
                q_part[rows], axis=0, keepdims=True
            )

    groups = width // (HEAD_GROUP * head_dim)
    ready = scored(0)
    for group in range(groups):
        following = scored(group + 1) if group + 1 < groups else None
        finished(group, *ready)
        ready = following

    value_sum = jnp.zeros((1, head_dim), f32)
    for slot in range(span):
        rows = pl.ds(slot * tokens, tokens)
        key_part = jnp.dot(d_score[rows, :], query_all[...], preferred_element_type=f32)
        value_part = jnp.dot(power[rows, :], grad_all[...], preferred_element_type=f32)
        partials[slot, :tokens, :head_dim] = key_part.astype(bf16)
        partials[slot, :tokens, head_dim:] = value_part.astype(bf16)
        value_sum += jnp.sum(value_part, axis=0, keepdims=True)
    sums[groups : groups + 1, :head_dim] = value_sum
    sums[groups : groups + 1, head_dim:] = jnp.zeros_like(value_sum)
    sums[groups + 1 :, :] = jnp.zeros((SUM_ROWS // 2 - groups - 1, pair), f32)
    high = sums[...].astype(bf16)
    low = (sums[...] - high.astype(f32)).astype(bf16)
    both_rows = jnp.concatenate([high, low], axis=0)
    for slot in range(span):
        partials[slot, tokens:, :] = both_rows


def attention(place, queries, out_grad, window, bias):
    tokens, width = queries.shape
    span, _, pair = window.shape
    head_dim = pair // 2
    reach = span * tokens
    vmem = pl.BlockSpec(memory_space=pltpu.VMEM)
    smem = pl.BlockSpec(memory_space=pltpu.SMEM)
    return pl.pallas_call(
        attention_kernel,
        out_shape=(
            jax.ShapeDtypeStruct((tokens, width), bf16),
            jax.ShapeDtypeStruct((tokens, width), f32),
            jax.ShapeDtypeStruct((span, tokens + SUM_ROWS, pair), bf16),
        ),
        in_specs=[smem] + [vmem] * 4,
        out_specs=(vmem,) * 3,
        scratch_shapes=[
            pltpu.VMEM((reach, head_dim), bf16),
            pltpu.VMEM((head_dim, reach), bf16),
            pltpu.VMEM((head_dim, reach), bf16),
            pltpu.VMEM((reach, tokens), f32),
            pltpu.VMEM((2, reach, HEAD_GROUP * tokens), f32),
            pltpu.VMEM((reach, width), bf16),
            pltpu.VMEM((reach, width), bf16),
            pltpu.VMEM((width, head_dim), bf16),
            pltpu.VMEM((width, head_dim), bf16),
            pltpu.VMEM((SUM_ROWS // 2, pair), f32),
        ],
        compiler_params=pltpu.CompilerParams(vmem_limit_bytes=40 * 1024 * 1024),
        cost_estimate=pl.CostEstimate(
            flops=12 * width * reach * tokens,
            bytes_accessed=4 * tokens * width * 2,
            transcendentals=reach * width,
        ),
        name="attention",
    )(place, queries, out_grad, window, bias)


def rotated(size, first):
    return [[(first + i) % size for i in range(size)]]


def exchanged(blocks, axis, first=0):
    return lax.all_to_all(
        blocks, axis, 0, 0, axis_index_groups=rotated(lax.axis_size(axis), first)
    )


def members_sum_kernel(received, copies):
    rows = jnp.sum(received[...].astype(f32), axis=0)
    rows = rows[: SUM_ROWS // 2] + rows[SUM_ROWS // 2 :]
    pair, width = received.shape[2], copies.shape[2]
    for start in range(0, width, pair):
        size = min(pair, width - start)
        part = rows[start // pair : start // pair + 1, :size]
        for copy in range(copies.shape[0]):
            copies[copy, :, start : start + size] = part


def members_sum(received, copies, width):
    span, rows, pair = received.shape
    return pl.pallas_call(
        members_sum_kernel,
        grid=(1,),
        out_shape=jax.ShapeDtypeStruct((copies, 1, width), f32),
        in_specs=[pl.BlockSpec((span, SUM_ROWS, pair), lambda i: (0, rows // SUM_ROWS - 1, 0))],
        out_specs=pl.BlockSpec((copies, 1, width), lambda i: (0, 0, 0)),
        name="members_sum",
    )(received)


def per_device(queries, keys, values, out_grad, q_bias, v_bias, doc_lengths):
    tokens, head_dim = keys.shape[1], keys.shape[2]
    width = queries.shape[2]
    groups = lax.axis_size("z") * lax.axis_size("y") // SPAN
    shard = lax.axis_index(SEQ)
    member = shard % SPAN
    place = jnp.concatenate([jnp.stack([shard, member]).astype(jnp.int32), doc_lengths[0]])
    bias = jnp.concatenate([q_bias, v_bias])[None]

    own = jnp.concatenate([keys[0], values[0]], axis=1)
    before = lax.ppermute(own, SEQ, [(i, i + SPAN) for i in range((groups - 1) * SPAN)])
    later = ((jnp.arange(SPAN) + MEMBER_FIRST) % SPAN >= member)[:, None, None]
    window = among_members(jnp.where(later, own[None], before[None]), groups)

    attended, q_grad, partials = attention(place, queries[0], out_grad[0], window, bias)

    received = among_members(partials, groups)
    copies = members_sum(received, lax.axis_size("rep"), width + head_dim)
    received = received[:, :tokens].astype(f32)
    mine = jnp.sum(jnp.where(later, received, 0.0), axis=0)
    others = jnp.sum(jnp.where(later, 0.0, received), axis=0).astype(bf16)
    returned = lax.ppermute(others, SEQ, [(i + SPAN, i) for i in range((groups - 1) * SPAN)])
    owned = mine + returned.astype(f32)

    rep_sums = jnp.sum(exchanged(copies, "rep"), axis=0)
    rep_sums, owned = lax.optimization_barrier((rep_sums, owned))
    copies = jnp.broadcast_to(rep_sums[None], (groups,) + rep_sums.shape)
    rows = along_groups(copies, groups)
    shards = groups * SPAN
    inverse = 1.0 / math.sqrt(shards * tokens * lax.axis_size("rep"))
    q_total = jnp.sum(rows[:, 0, :width], axis=0) * inverse
    v_total = jnp.sum(rows[:, 0, width:], axis=0) * inverse
    return (
        attended[None],
        q_grad[None],
        owned[None, :, :head_dim],
        owned[None, :, head_dim:],
        q_total,
        v_total,
    )


def among_members(blocks, groups):
    order = rotated(SPAN, MEMBER_FIRST)[0]
    return lax.all_to_all(
        blocks, SEQ, 0, 0, axis_index_groups=[[g * SPAN + m for m in order] for g in range(groups)]
    )


def along_groups(blocks, groups):
    order = rotated(groups, groups * LINE_FIRST // 8)[0]
    return lax.all_to_all(
        blocks, SEQ, 0, 0, axis_index_groups=[[g * SPAN + m for g in order] for m in range(SPAN)]
    )


def solution(mesh):
    seq, rep = mesh.shape["seq"], mesh.shape["rep"]
    fine = Mesh(mesh.devices.reshape(2 * seq // SPAN, SPAN // 2, rep), ("z", "y", "rep"))
    tokens = P("rep", SEQ, None)
    return jax.shard_map(
        per_device,
        mesh=fine,
        in_specs=(tokens, tokens, tokens, tokens, P(), P(), P("rep", None)),
        out_specs=(tokens, tokens, tokens, tokens, P(), P()),
        check_vma=False,
    )
```

time: 100 us -> 81.8 us (0.82)
  the two profiles are of different devices: /device:TPU:2 before, /device:TPU:1 now
where the time goes in v3:
time: 81.8 us; the launch traced here: 81.3 us
  starting transfers between devices  30.6 us (37%)
  blocking collectives  26 us (32%)
  waiting for transfers between devices  11.6 us (14%)
  Pallas kernels  7.14 us (9%)
  other arithmetic  3.26 us (4%)
  local copies, waits for them, and re-layouts  1.97 us (2%)
    all_to_all x1, starting transfers between devices, along_groups(): lax.all_to_all(blocks, SEQ, 0, 0, axis_index_groups=[[g * SPAN + m for g...  17 us
    all_to_all x1, blocking collectives, among_members(): lax.all_to_all(blocks, SEQ, 0, 0, axis_index_groups=[[g * SPAN + m for m...  14.6 us
    all_to_all x1, blocking collectives, exchanged(): lax.all_to_all(blocks, axis, 0, 0, axis_index_groups=rotated(lax.axis_siz...  11.4 us
    all_to_all x1, waiting for transfers between devices, among_members(): lax.all_to_all(blocks, SEQ, 0, 0, axis_index_groups=[[g * SPAN + m for m...  6.76 us
    all_to_all x1, starting transfers between devices, among_members(): lax.all_to_all(blocks, SEQ, 0, 0, axis_index_groups=[[g * SPAN + m for m...  6.63 us
    ppermute x1, starting transfers between devices, per_device(): lax.ppermute(own, SEQ, [(i, i + SPAN) for i in range((groups - 1) * SPAN)])  5.72 us
    pallas_call x1, Pallas kernels, attention(): pl.pallas_call(attention_kernel, out_shape=(jax.ShapeDtypeStruct((tokens,...  5.66 us
    all_to_all x1, waiting for transfers between devices, along_groups(): lax.all_to_all(blocks, SEQ, 0, 0, axis_index_groups=[[g * SPAN + m for g...  3.53 us
  transfers between devices with their start and end apart: 4, of which 3 were waited for; matrix products, arithmetic and copies ran while one was open for 1% of the time, Pallas kernels for 2%

profile of v3, /device:TPU:1, one launch (start us, length us, event | category | flops | bytes accessed | tf_op | source)
XLA Modules:
  0.0 81.3 jit_solution(4512476714905752143)
XLA Ops:
  0.6 0.8 pad_maximum_fusion
  1.4 5.7 %collective-permute-start = (bf16[128,256]{1,0:T(8,128)(2,1)S(1)}, bf16[128,256]{1,0:T(8,128)(2,1)S(1)}, u32[]{:S(2)}, u32[]{:S(2)}) collective-permute-start(bf16[128,256]{1,0:T(8,128)(2,1)S(1)} %pad_maximum_fusion), channel_id=1, source_target_pairs={{0,64},{8,72},{16,80},{24,88},{32,96},{40,104},{48,112},{56,120},{... | collective-permute-start | bytes 196616 | tf_op jit(solution)/shard_map/ppermute | solution.py:212
  7.2 1.3 %collective-permute-done = bf16[128,256]{1,0:T(8,128)(2,1)S(1)} collective-permute-done((bf16[128,256]{1,0:T(8,128)(2,1)S(1)}, bf16[128,256]{1,0:T(8,128)(2,1)S(1)}, u32[]{:S(2)}, u32[]{:S(2)}) %collective-permute-start) | collective-permute-done | bytes 65568 | tf_op jit(solution)/shard_map/ppermute | solution.py:212
  8.5 0.9 %broadcast_select_fusion = bf16[8,128,256]{2,1,0:T(8,128)(2,1)} fusion(pred[8]{0:T(512)(128)(4,1)S(1)} %fusion.2, bf16[128,256]{1,0:T(8,128)(2,1)S(1)} %collective-permute-done, bf16[128,256]{1,0:T(8,128)(2,1)S(1)} %pad_maximum_fusion), kind=kLoop, calls=%fused_computation.4 | loop fusion | flops 262144 | bytes 655368 | tf_op jit(solution)/shard_map/jit(_where)/select_n | solution.py:214
  9.4 6.6 %all-to-all-start = ((bf16[8,128,256]{2,1,0:T(8,128)(2,1)}), bf16[8,128,256]{2,1,0:T(8,128)(2,1)S(1)}, u32[]{:S(2)}, u32[]{:S(2)}) async-start(bf16[8,128,256]{2,1,0:T(8,128)(2,1)} %broadcast_select_fusion), calls=%async_computation | async-start | bytes 1048576 | tf_op jit(solution)/shard_map/all_to_all | solution.py:246
  16.0 0.0 copy-done.3
  16.0 0.0 copy-start.5
  16.0 0.6 copy-done.5
  16.7 0.1 pad_add_fusion.place
  16.8 6.8 %all-to-all-done.window = bf16[8,128,256]{2,1,0:T(8,128)(2,1)S(1)} async-done(((bf16[8,128,256]{2,1,0:T(8,128)(2,1)}), bf16[8,128,256]{2,1,0:T(8,128)(2,1)S(1)}, u32[]{:S(2)}, u32[]{:S(2)}) %all-to-all-start) | async-done | bytes 524320 | tf_op jit(solution)/shard_map/all_to_all | solution.py:246
  23.5 0.0 copy-done
  23.5 5.7 %attention.1 = (bf16[128,1024]{1,0:T(8,128)(2,1)}, f32[128,1024]{1,0:T(8,128)}, bf16[8,144,256]{2,1,0:T(8,128)(2,1)S(1)}) custom-call(s32[18]{0:T(128)S(1)} %pad_add_fusion.place, bf16[128,1024]{1,0:T(8,128)(2,1)S(1)} %bitcast.14, bf16[128,1024]{1,0:T(8,128)(2,1)S(1)} %bitcast.15, bf16[8,128,256]{2,1,0:T(8,128)(2,1)S(1)} %all-to-all-done.window, ...), custom_call_target="tpu_custom_call" | custom-call | flops 1610612736 | bytes 1048576 | tf_op jit(solution)/shard_map/attention/pallas_call | solution.py:138
  29.2 14.6 %all_to_all.20.received = bf16[8,144,256]{2,1,0:T(8,128)(2,1)S(1)} all-to-all(bf16[8,144,256]{2,1,0:T(8,128)(2,1)S(1)} %get-tuple-element.13), channel_id=1, replica_groups={{0,8,16,24,32,40,48,56},{64,72,80,88,96,104,112,120},{128,136,144,152,1..., dimensions={0} | all-to-all | bytes 1179648 | tf_op jit(solution)/shard_map/all_to_all | solution.py:246
  43.8 0.3 fusion.1
  44.1 1.3 %collective-permute-start.1 = (bf16[128,256]{1,0:T(8,128)(2,1)S(1)}, bf16[128,256]{1,0:T(8,128)(2,1)S(1)}, u32[]{:S(2)}, u32[]{:S(2)}) collective-permute-start(bf16[128,256]{1,0:T(8,128)(2,1)S(1)} %get-tuple-element.16), channel_id=1, source_target_pairs={{64,0},{72,8},{80,16},{88,24},{96,32},{104,40},{112,48},{120,56},{... | collective-permute-start | bytes 196616 | tf_op jit(solution)/shard_map/ppermute | solution.py:223
  45.4 1.5 %members_sum.1 = f32[8,1,1152]{2,1,0:T(1,128)} custom-call(bf16[8,144,256]{2,1,0:T(8,128)(2,1)} %copy-done.2), custom_call_target="tpu_custom_call" | custom-call | tf_op jit(solution)/shard_map/members_sum/pallas_call | solution.py:192
  46.9 11.4 %all_to_all.21 = f32[8,1,1152]{2,1,0:T(1,128)S(1)} all-to-all(f32[8,1,1152]{2,1,0:T(1,128)} %members_sum.1), channel_id=1, replica_groups={{0,1,2,3,4,5,6,7},{8,9,10,11,12,13,14,15},{16,17,18,19,20,21,22,23},{24..., dimensions={0} | all-to-all | bytes 73728 | tf_op jit(solution)/shard_map/all_to_all | solution.py:174
  58.3 0.0 collective-permute-done.1
  58.3 0.6 broadcast_in_dim.78
  59.0 17.0 %all-to-all-start.3 = ((f32[8,1,1152]{2,1,0:T(1,128)}), f32[8,1,1152]{2,1,0:T(1,128)S(1)}, u32[]{:S(2)}, u32[]{:S(2)}) async-start(f32[8,1,1152]{2,1,0:T(1,128)} %broadcast_in_dim.78), calls=%async_computation.3 | async-start | bytes 73728 | tf_op jit(solution)/shard_map/all_to_all | solution.py:253
  75.9 0.7 slice_bitcast_fusion
  76.6 3.5 %all-to-all-done.3 = f32[8,1,1152]{2,1,0:T(1,128)S(1)} async-done(((f32[8,1,1152]{2,1,0:T(1,128)}), f32[8,1,1152]{2,1,0:T(1,128)S(1)}, u32[]{:S(2)}, u32[]{:S(2)}) %all-to-all-start.3) | async-done | bytes 36896 | tf_op jit(solution)/shard_map/all_to_all | solution.py:253
  80.2 0.6 broadcast_multiply_fusion
  80.8 0.5 broadcast_multiply_fusion.1
  (18 shorter events, 0.2 us)
Async XLA Ops:
  1.4 7.0 %collective-permute-start = (bf16[128,256]{1,0:T(8,128)(2,1)S(1)}, bf16[128,256]{1,0:T(8,128)(2,1)S(1)}, u32[]{:S(2)}, u32[]{:S(2)}) collective-permute-start(bf16[128,256]{1,0:T(8,128)(2,1)S(1)} %pad_maximum_fusion), channel_id=1, source_target_pairs={{0,64},{8,72},{16,80},{24,88},{32,96},{40,104},{48,112},{56,120},{... | collective-permute-start | bytes 196616 | tf_op jit(solution)/shard_map/ppermute | solution.py:212
  9.4 6.6 %copy-start.3 = (f32[1024]{0:T(1024)S(1)}, f32[1024]{0:T(1024)}, u32[]{:S(2)}) copy-start(f32[1024]{0:T(1024)} %param.11) | copy-start | bytes 12292
  9.4 6.6 %copy-start.4 = (f32[128]{0:T(128)S(1)}, f32[128]{0:T(128)}, u32[]{:S(2)}) copy-start(f32[128]{0:T(128)} %param.12) | copy-start | bytes 1540
  9.4 14.2 %copy-start = (bf16[1,128,1024]{2,1,0:T(8,128)(2,1)S(1)}, bf16[1,128,1024]{2,1,0:T(8,128)(2,1)}, u32[]{:S(2)}) copy-start(bf16[1,128,1024]{2,1,0:T(8,128)(2,1)} %param.7) | copy-start | bytes 786436
  9.4 14.2 %copy-start.1 = (bf16[1,128,1024]{2,1,0:T(8,128)(2,1)S(1)}, bf16[1,128,1024]{2,1,0:T(8,128)(2,1)}, u32[]{:S(2)}) copy-start(bf16[1,128,1024]{2,1,0:T(8,128)(2,1)} %param.10) | copy-start | bytes 786436
  9.4 14.2 %all-to-all-start = ((bf16[8,128,256]{2,1,0:T(8,128)(2,1)}), bf16[8,128,256]{2,1,0:T(8,128)(2,1)S(1)}, u32[]{:S(2)}, u32[]{:S(2)}) async-start(bf16[8,128,256]{2,1,0:T(8,128)(2,1)} %broadcast_select_fusion), calls=%async_computation | async-start | bytes 1048576 | tf_op jit(solution)/shard_map/all_to_all | solution.py:246
  16.0 0.7 copy-start.5
  43.8 1.6 %copy-start.2 = (bf16[8,144,256]{2,1,0:T(8,128)(2,1)}, bf16[8,144,256]{2,1,0:T(8,128)(2,1)S(1)}, u32[]{:S(2)}) copy-start(bf16[8,144,256]{2,1,0:T(8,128)(2,1)S(1)} %all_to_all.20.received) | copy-start | bytes 1769476
  44.1 14.2 %collective-permute-start.1 = (bf16[128,256]{1,0:T(8,128)(2,1)S(1)}, bf16[128,256]{1,0:T(8,128)(2,1)S(1)}, u32[]{:S(2)}, u32[]{:S(2)}) collective-permute-start(bf16[128,256]{1,0:T(8,128)(2,1)S(1)} %get-tuple-element.16), channel_id=1, source_target_pairs={{64,0},{72,8},{80,16},{88,24},{96,32},{104,40},{112,48},{120,56},{... | collective-permute-start | bytes 196616 | tf_op jit(solution)/shard_map/ppermute | solution.py:223
  59.0 21.2 %all-to-all-start.3 = ((f32[8,1,1152]{2,1,0:T(1,128)}), f32[8,1,1152]{2,1,0:T(1,128)S(1)}, u32[]{:S(2)}, u32[]{:S(2)}) async-start(f32[8,1,1152]{2,1,0:T(1,128)} %broadcast_in_dim.78), calls=%async_computation.3 | async-start | bytes 73728 | tf_op jit(solution)/shard_map/all_to_all | solution.py:253

commit v4 on v3

--- a/solution.py
+++ b/solution.py
@@ -12,8 +12,9 @@
 SPAN = 8
 HEAD_GROUP = 2
 SEQ = ("z", "y")
-MEMBER_FIRST = 0
+MEMBER_FIRST = 7
 LINE_FIRST = 5
+REP_FIRST = 7
 SUM_ROWS = 16
 masked_fill = -1e30
 f32 = jnp.float32
@@ -176,29 +177,6 @@
     )
 
 
-def members_sum_kernel(received, copies):
-    rows = jnp.sum(received[...].astype(f32), axis=0)
-    rows = rows[: SUM_ROWS // 2] + rows[SUM_ROWS // 2 :]
-    pair, width = received.shape[2], copies.shape[2]
-    for start in range(0, width, pair):
-        size = min(pair, width - start)
-        part = rows[start // pair : start // pair + 1, :size]
-        for copy in range(copies.shape[0]):
-            copies[copy, :, start : start + size] = part
-
-
-def members_sum(received, copies, width):
-    span, rows, pair = received.shape
-    return pl.pallas_call(
-        members_sum_kernel,
-        grid=(1,),
-        out_shape=jax.ShapeDtypeStruct((copies, 1, width), f32),
-        in_specs=[pl.BlockSpec((span, SUM_ROWS, pair), lambda i: (0, rows // SUM_ROWS - 1, 0))],
-        out_specs=pl.BlockSpec((copies, 1, width), lambda i: (0, 0, 0)),
-        name="members_sum",
-    )(received)
-
-
 def per_device(queries, keys, values, out_grad, q_bias, v_bias, doc_lengths):
     tokens, head_dim = keys.shape[1], keys.shape[2]
     width = queries.shape[2]
@@ -211,31 +189,37 @@
     own = jnp.concatenate([keys[0], values[0]], axis=1)
     before = lax.ppermute(own, SEQ, [(i, i + SPAN) for i in range((groups - 1) * SPAN)])
     later = ((jnp.arange(SPAN) + MEMBER_FIRST) % SPAN >= member)[:, None, None]
+    before, place, bias = lax.optimization_barrier((before, place, bias))
     window = among_members(jnp.where(later, own[None], before[None]), groups)
 
     attended, q_grad, partials = attention(place, queries[0], out_grad[0], window, bias)
 
     received = among_members(partials, groups)
-    copies = members_sum(received, lax.axis_size("rep"), width + head_dim)
+    sums = jnp.sum(received[:, tokens:].astype(f32), axis=0)
+    sums = sums[: SUM_ROWS // 2] + sums[SUM_ROWS // 2 :]
+    copies = jnp.broadcast_to(sums[None], (lax.axis_size("rep"),) + sums.shape)
     received = received[:, :tokens].astype(f32)
     mine = jnp.sum(jnp.where(later, received, 0.0), axis=0)
     others = jnp.sum(jnp.where(later, 0.0, received), axis=0).astype(bf16)
     returned = lax.ppermute(others, SEQ, [(i + SPAN, i) for i in range((groups - 1) * SPAN)])
     owned = mine + returned.astype(f32)
 
-    rep_sums = jnp.sum(exchanged(copies, "rep"), axis=0)
-    rep_sums, owned = lax.optimization_barrier((rep_sums, owned))
+    rep_sums = jnp.sum(exchanged(copies, "rep", REP_FIRST), axis=0)
+    k_grad, v_grad = owned[None, :, :head_dim], owned[None, :, head_dim:]
+    rep_sums, k_grad, v_grad = lax.optimization_barrier((rep_sums, k_grad, v_grad))
     copies = jnp.broadcast_to(rep_sums[None], (groups,) + rep_sums.shape)
     rows = along_groups(copies, groups)
     shards = groups * SPAN
     inverse = 1.0 / math.sqrt(shards * tokens * lax.axis_size("rep"))
-    q_total = jnp.sum(rows[:, 0, :width], axis=0) * inverse
-    v_total = jnp.sum(rows[:, 0, width:], axis=0) * inverse
+    totals = jnp.sum(rows, axis=0) * inverse
+    full = width // (2 * head_dim)
+    q_total = totals[:full].reshape(width)
+    v_total = totals[full, :head_dim]
     return (
         attended[None],
         q_grad[None],
-        owned[None, :, :head_dim],
-        owned[None, :, head_dim:],
+        k_grad,
+        v_grad,
         q_total,
         v_total,
     )

time: 81.8 us -> 75.5 us (0.923)
  blocking collectives: 26 us -> 57.1 us
  starting transfers between devices: 30.6 us -> 7.01 us
  waiting for transfers between devices: 11.6 us -> 0.01 us
  other arithmetic: 3.26 us -> 1.3 us
  Pallas kernels: 7.14 us -> 5.69 us
  local copies, waits for them, and re-layouts: 1.97 us -> 3.11 us
    all_to_all x2 -> x0, starting transfers between devices: 23.6 us -> none  [the longest x1 17 us: along_groups(): lax.all_to_all(blocks, SEQ, 0, 0, axis_index_groups=[[g * SPAN + m for g...]
    all_to_all x0 -> x1, blocking collectives: none -> 21.4 us  [along_groups(): lax.all_to_all(blocks, SEQ, 0, 0, axis_index_groups=[[g * SPAN + m for g...]
    all_to_all x2 -> x0, waiting for transfers between devices: 10.3 us -> none  [the longest x1 6.76 us: among_members(): lax.all_to_all(blocks, SEQ, 0, 0, axis_index_groups=[[g * SPAN + m for m...]
    all_to_all x1 -> x2, blocking collectives: 14.6 us -> 24.8 us  [among_members(): lax.all_to_all(blocks, SEQ, 0, 0, axis_index_groups=[[g * SPAN + m for m...]
    pallas_call x1 -> x0, Pallas kernels: 1.49 us -> none  [members_sum(): pl.pallas_call(members_sum_kernel, grid=(1,), out_shape=jax.ShapeDtypeStr...]
    ppermute x1, waiting for transfers between devices: 1.28 us -> 0.01 us  [per_device(): lax.ppermute(own, SEQ, [(i, i + SPAN) for i in range((groups - 1) * SPAN)])]
    unnamed x12, local copies, waits for them, and re-layouts: 0.67 us -> 1.92 us
    mul x2 -> x1, other arithmetic: 1.11 us -> 0.01 us  [per_device(): totals = jnp.sum(rows, axis=0) * inverse]
  transfers between devices with their start and end apart: 4 -> 2, of which waited for: 3 -> 0; matrix products, arithmetic and copies ran while one was open for 1% -> 0% of each run, Pallas kernels for 2% -> 0%
where the time goes in v4:
time: 75.5 us; the launch traced here: 75 us
  blocking collectives  57.1 us (76%)
  starting transfers between devices  7.01 us (9%)
  Pallas kernels  5.69 us (8%)
  local copies, waits for them, and re-layouts  3.11 us (4%)
  other arithmetic  1.3 us (2%)
  between operations  0.78 us (1%)
    all_to_all x2, blocking collectives, among_members(): lax.all_to_all(blocks, SEQ, 0, 0, axis_index_groups=[[g * SPAN + m for m...  24.8 us
    all_to_all x1, blocking collectives, along_groups(): lax.all_to_all(blocks, SEQ, 0, 0, axis_index_groups=[[g * SPAN + m for g...  21.4 us
    all_to_all x1, blocking collectives, exchanged(): lax.all_to_all(blocks, axis, 0, 0, axis_index_groups=rotated(lax.axis_siz...  10.9 us
    ppermute x1, starting transfers between devices, per_device(): lax.ppermute(own, SEQ, [(i, i + SPAN) for i in range((groups - 1) * SPAN)])  5.72 us
    pallas_call x1, Pallas kernels, attention(): pl.pallas_call(attention_kernel, out_shape=(jax.ShapeDtypeStruct((tokens,...  5.69 us
    unnamed x12, local copies, waits for them, and re-layouts  1.92 us
  transfers between devices with their start and end apart: 2, of which 0 were waited for; matrix products, arithmetic and copies ran while one was open for 0% of the time, Pallas kernels for 0%

profile of v4, /device:TPU:1, one launch (start us, length us, event | category | flops | bytes accessed | tf_op | source)
XLA Modules:
  0.0 75.0 jit_solution(14880010892174950140)
XLA Ops:
  0.6 0.8 %pad_maximum_fusion = bf16[128,256]{1,0:T(8,128)(2,1)S(1)} fusion(bf16[128,128]{1,0:T(8,128)(2,1)} %bitcast.20, bf16[128,128]{1,0:T(8,128)(2,1)} %bitcast.21), kind=kLoop, calls=%fused_computation.9 | loop fusion | flops 131072 | bytes 131072 | tf_op jit(solution)/shard_map/concatenate | solution.py:189
  1.4 5.7 %collective-permute-start = (bf16[128,256]{1,0:T(8,128)(2,1)S(1)}, bf16[128,256]{1,0:T(8,128)(2,1)S(1)}, u32[]{:S(2)}, u32[]{:S(2)}) collective-permute-start(bf16[128,256]{1,0:T(8,128)(2,1)S(1)} %pad_maximum_fusion), channel_id=1, source_target_pairs={{0,64},{8,72},{16,80},{24,88},{32,96},{40,104},{48,112},{56,120},{... | collective-permute-start | bytes 196616 | tf_op jit(solution)/shard_map/ppermute | solution.py:190
  7.2 0.0 copy-start.2
  7.2 0.0 copy-start.3
  7.2 0.6 copy-done.2
  7.8 0.0 copy-done.3
  7.9 0.0 copy-start.4
  7.9 0.6 copy-done.4
  8.5 0.1 pad_add_fusion.place
  8.6 0.0 collective-permute-done
  8.6 0.1 broadcast_select_fusion
  8.7 0.0 copy-start
  8.7 0.0 copy-start.1
  8.7 13.3 %all_to_all.20.window = bf16[8,128,256]{2,1,0:T(8,128)(2,1)S(1)} all-to-all(bf16[8,128,256]{2,1,0:T(8,128)(2,1)S(1)} %broadcast_select_fusion), channel_id=1, replica_groups={{56,0,8,16,24,32,40,48},{120,64,72,80,88,96,104,112},{184,128,136,144,1..., dimensions={0} | all-to-all | bytes 1048576 | tf_op jit(solution)/shard_map/all_to_all | solution.py:230
  22.0 5.7 %attention.1 = (bf16[128,1024]{1,0:T(8,128)(2,1)}, f32[128,1024]{1,0:T(8,128)}, bf16[8,144,256]{2,1,0:T(8,128)(2,1)S(1)}) custom-call(s32[18]{0:T(128)S(1)} %pad_add_fusion.place, bf16[128,1024]{1,0:T(8,128)(2,1)S(1)} %bitcast.18, bf16[128,1024]{1,0:T(8,128)(2,1)S(1)} %bitcast.19, bf16[8,128,256]{2,1,0:T(8,128)(2,1)S(1)} %all_to_all.20.window, ...), custom_call_target="tpu_custom_call" | custom-call | flops 1610612736 | bytes 1048576 | tf_op jit(solution)/shard_map/attention/pallas_call | solution.py:139
  27.7 11.5 %all_to_all.21 = bf16[8,144,256]{2,1,0:T(8,128)(2,1)S(1)} all-to-all(bf16[8,144,256]{2,1,0:T(8,128)(2,1)S(1)} %get-tuple-element.20), channel_id=1, replica_groups={{56,0,8,16,24,32,40,48},{120,64,72,80,88,96,104,112},{184,128,136,144,1..., dimensions={0} | all-to-all | bytes 1179648 | tf_op jit(solution)/shard_map/all_to_all | solution.py:230
  39.2 0.3 fusion.1
  39.5 1.3 %collective-permute-start.1 = (bf16[128,256]{1,0:T(8,128)(2,1)S(1)}, bf16[128,256]{1,0:T(8,128)(2,1)S(1)}, u32[]{:S(2)}, u32[]{:S(2)}) collective-permute-start(bf16[128,256]{1,0:T(8,128)(2,1)S(1)} %get-tuple-element.24), channel_id=1, source_target_pairs={{64,0},{72,8},{80,16},{88,24},{96,32},{104,40},{112,48},{120,56},{... | collective-permute-start | bytes 196616 | tf_op jit(solution)/shard_map/ppermute | solution.py:204
  40.8 10.9 %all_to_all.22 = f32[8,8,256]{2,1,0:T(8,128)S(1)} all-to-all(f32[8,8,256]{2,1,0:T(8,128)S(1)} %broadcast_in_dim.78), channel_id=1, replica_groups={{7,0,1,2,3,4,5,6},{15,8,9,10,11,12,13,14},{23,16,17,18,19,20,21,22},{31..., dimensions={0} | all-to-all | bytes 131072 | tf_op jit(solution)/shard_map/all_to_all | solution.py:175
  51.8 0.0 collective-permute-done.1
  51.8 0.7 slice_bitcast_fusion
  52.5 21.4 %all_to_all.23 = f32[8,8,256]{2,1,0:T(8,128)S(1)} all-to-all(f32[8,8,256]{2,1,0:T(8,128)S(1)} %broadcast_in_dim.82), channel_id=1, replica_groups={{320,384,448,0,64,128,192,256},{328,392,456,8,72,136,200,264},{336,400,..., dimensions={0} | all-to-all | bytes 131072 | tf_op jit(solution)/shard_map/all_to_all | solution.py:237
  73.9 0.5 slice_bitcast_fusion.3
  74.4 0.6 copy.13
  (14 shorter events, 0.1 us)
Async XLA Ops:
  1.4 7.2 %collective-permute-start = (bf16[128,256]{1,0:T(8,128)(2,1)S(1)}, bf16[128,256]{1,0:T(8,128)(2,1)S(1)}, u32[]{:S(2)}, u32[]{:S(2)}) collective-permute-start(bf16[128,256]{1,0:T(8,128)(2,1)S(1)} %pad_maximum_fusion), channel_id=1, source_target_pairs={{0,64},{8,72},{16,80},{24,88},{32,96},{40,104},{48,112},{56,120},{... | collective-permute-start | bytes 196616 | tf_op jit(solution)/shard_map/ppermute | solution.py:190
  7.2 0.7 copy-start.2
  7.2 0.7 copy-start.3
  7.9 0.7 copy-start.4
  8.7 13.3 %copy-start = (bf16[1,128,1024]{2,1,0:T(8,128)(2,1)S(1)}, bf16[1,128,1024]{2,1,0:T(8,128)(2,1)}, u32[]{:S(2)}) copy-start(bf16[1,128,1024]{2,1,0:T(8,128)(2,1)} %param.7) | copy-start | bytes 786436
  8.7 13.3 %copy-start.1 = (bf16[1,128,1024]{2,1,0:T(8,128)(2,1)S(1)}, bf16[1,128,1024]{2,1,0:T(8,128)(2,1)}, u32[]{:S(2)}) copy-start(bf16[1,128,1024]{2,1,0:T(8,128)(2,1)} %param.10) | copy-start | bytes 786436
  39.5 12.3 %collective-permute-start.1 = (bf16[128,256]{1,0:T(8,128)(2,1)S(1)}, bf16[128,256]{1,0:T(8,128)(2,1)S(1)}, u32[]{:S(2)}, u32[]{:S(2)}) collective-permute-start(bf16[128,256]{1,0:T(8,128)(2,1)S(1)} %get-tuple-element.24), channel_id=1, source_target_pairs={{64,0},{72,8},{80,16},{88,24},{96,32},{104,40},{112,48},{120,56},{... | collective-permute-start | bytes 196616 | tf_op jit(solution)/shard_map/ppermute | solution.py:204

commit v5 on v4

--- a/solution.py
+++ b/solution.py
@@ -10,7 +10,7 @@
 from jax.sharding import PartitionSpec as P
 
 SPAN = 8
-HEAD_GROUP = 2
+HEAD_GROUP = 4
 SEQ = ("z", "y")
 MEMBER_FIRST = 7
 LINE_FIRST = 5
@@ -67,7 +67,7 @@
         for slot in range(span):
             rows = pl.ds(slot * tokens, tokens)
             part = transposed_product(window[slot, :, :head_dim], query_rows)
-            part = part * (scale * math.log2(math.e)) + jnp.concatenate([fill[rows, :]] * 2, axis=1)
+            part = part * (scale * math.log2(math.e)) + jnp.concatenate([fill[rows, :]] * HEAD_GROUP, axis=1)
             score[group % 2, rows, :] = part
             top = jnp.maximum(top, jnp.max(part.reshape(tokens // 8, 8, both), axis=0))
         return query_rows, grad_rows, jnp.max(top, axis=0, keepdims=True)
@@ -100,8 +100,9 @@
             rows = slice(n * tokens, (n + 1) * tokens)
             attended[:, c] = found[rows]
             q_grad[:, c] = q_part[rows]
-            sums[group : group + 1, n * head_dim : (n + 1) * head_dim] = jnp.sum(
-                q_part[rows], axis=0, keepdims=True
+            head = group * HEAD_GROUP + n
+            sums[head // 2 : head // 2 + 1, head % 2 * head_dim : (head % 2 + 1) * head_dim] = (
+                jnp.sum(q_part[rows], axis=0, keepdims=True)
             )
 
     groups = width // (HEAD_GROUP * head_dim)
@@ -119,9 +120,10 @@
         partials[slot, :tokens, :head_dim] = key_part.astype(bf16)
         partials[slot, :tokens, head_dim:] = value_part.astype(bf16)
         value_sum += jnp.sum(value_part, axis=0, keepdims=True)
-    sums[groups : groups + 1, :head_dim] = value_sum
-    sums[groups : groups + 1, head_dim:] = jnp.zeros_like(value_sum)
-    sums[groups + 1 :, :] = jnp.zeros((SUM_ROWS // 2 - groups - 1, pair), f32)
+    full = width // pair
+    sums[full : full + 1, :head_dim] = value_sum
+    sums[full : full + 1, head_dim:] = jnp.zeros_like(value_sum)
+    sums[full + 1 :, :] = jnp.zeros((SUM_ROWS // 2 - full - 1, pair), f32)
     high = sums[...].astype(bf16)
     low = (sums[...] - high.astype(f32)).astype(bf16)
     both_rows = jnp.concatenate([high, low], axis=0)
@@ -197,24 +199,25 @@
     received = among_members(partials, groups)
     sums = jnp.sum(received[:, tokens:].astype(f32), axis=0)
     sums = sums[: SUM_ROWS // 2] + sums[SUM_ROWS // 2 :]
+    full = width // (2 * head_dim)
+    sums = jnp.concatenate([sums[:full], sums[full : 2 * full, :head_dim]], axis=1)
     copies = jnp.broadcast_to(sums[None], (lax.axis_size("rep"),) + sums.shape)
     received = received[:, :tokens].astype(f32)
     mine = jnp.sum(jnp.where(later, received, 0.0), axis=0)
     others = jnp.sum(jnp.where(later, 0.0, received), axis=0).astype(bf16)
     returned = lax.ppermute(others, SEQ, [(i + SPAN, i) for i in range((groups - 1) * SPAN)])
-    owned = mine + returned.astype(f32)
 
     rep_sums = jnp.sum(exchanged(copies, "rep", REP_FIRST), axis=0)
-    k_grad, v_grad = owned[None, :, :head_dim], owned[None, :, head_dim:]
+    k_grad = mine[None, :, :head_dim] + returned[None, :, :head_dim].astype(f32)
+    v_grad = mine[None, :, head_dim:] + returned[None, :, head_dim:].astype(f32)
     rep_sums, k_grad, v_grad = lax.optimization_barrier((rep_sums, k_grad, v_grad))
     copies = jnp.broadcast_to(rep_sums[None], (groups,) + rep_sums.shape)
     rows = along_groups(copies, groups)
     shards = groups * SPAN
     inverse = 1.0 / math.sqrt(shards * tokens * lax.axis_size("rep"))
     totals = jnp.sum(rows, axis=0) * inverse
-    full = width // (2 * head_dim)
-    q_total = totals[:full].reshape(width)
-    v_total = totals[full, :head_dim]
+    q_total = totals[:, : 2 * head_dim].reshape(width)
+    v_total = totals[0, 2 * head_dim :]
     return (
         attended[None],
         q_grad[None],

time: 75.5 us -> 74.8 us (level)
  no operation moved by 1% of the time
where the time goes in v5:
time: 74.8 us; the launch traced here: 74.4 us
  blocking collectives  56.9 us (76%)
  starting transfers between devices  7.01 us (9%)
  Pallas kernels  5.24 us (7%)
  local copies, waits for them, and re-layouts  2.46 us (3%)
  other arithmetic  1.98 us (3%)
  between operations  0.79 us (1%)
    all_to_all x2, blocking collectives, among_members(): lax.all_to_all(blocks, SEQ, 0, 0, axis_index_groups=[[g * SPAN + m for m...  24.8 us
    all_to_all x1, blocking collectives, along_groups(): lax.all_to_all(blocks, SEQ, 0, 0, axis_index_groups=[[g * SPAN + m for g...  21.3 us
    all_to_all x1, blocking collectives, exchanged(): lax.all_to_all(blocks, axis, 0, 0, axis_index_groups=rotated(lax.axis_siz...  10.9 us
    ppermute x1, starting transfers between devices, per_device(): lax.ppermute(own, SEQ, [(i, i + SPAN) for i in range((groups - 1) * SPAN)])  5.72 us
    pallas_call x1, Pallas kernels, attention(): pl.pallas_call(attention_kernel, out_shape=(jax.ShapeDtypeStruct((tokens,...  5.24 us
    unnamed x12, local copies, waits for them, and re-layouts  1.92 us
  transfers between devices with their start and end apart: 2, of which 0 were waited for; matrix products, arithmetic and copies ran while one was open for 0% of the time, Pallas kernels for 0%

profile of v5, /device:TPU:1, one launch (start us, length us, event | category | flops | bytes accessed | tf_op | source)
XLA Modules:
  0.0 74.4 jit_solution(2607904862711166572)
XLA Ops:
  0.6 0.8 %pad_maximum_fusion = bf16[128,256]{1,0:T(8,128)(2,1)S(1)} fusion(bf16[128,128]{1,0:T(8,128)(2,1)} %bitcast.20, bf16[128,128]{1,0:T(8,128)(2,1)} %bitcast.21), kind=kLoop, calls=%fused_computation.10 | loop fusion | flops 131072 | bytes 131072 | tf_op jit(solution)/shard_map/concatenate | solution.py:191
  1.4 5.7 %collective-permute-start = (bf16[128,256]{1,0:T(8,128)(2,1)S(1)}, bf16[128,256]{1,0:T(8,128)(2,1)S(1)}, u32[]{:S(2)}, u32[]{:S(2)}) collective-permute-start(bf16[128,256]{1,0:T(8,128)(2,1)S(1)} %pad_maximum_fusion), channel_id=1, source_target_pairs={{0,64},{8,72},{16,80},{24,88},{32,96},{40,104},{48,112},{56,120},{... | collective-permute-start | bytes 196616 | tf_op jit(solution)/shard_map/ppermute | solution.py:192
  7.2 0.0 copy-start.2
  7.2 0.0 copy-start.3
  7.2 0.6 copy-done.2
  7.8 0.0 copy-done.3
  7.9 0.0 copy-start.4
  7.9 0.6 copy-done.4
  8.5 0.1 pad_add_fusion.place
  8.6 0.0 collective-permute-done
  8.6 0.1 broadcast_select_fusion
  8.7 0.0 copy-start
  8.7 0.0 copy-start.1
  8.7 13.3 %all_to_all.20.window = bf16[8,128,256]{2,1,0:T(8,128)(2,1)S(1)} all-to-all(bf16[8,128,256]{2,1,0:T(8,128)(2,1)S(1)} %broadcast_select_fusion), channel_id=1, replica_groups={{56,0,8,16,24,32,40,48},{120,64,72,80,88,96,104,112},{184,128,136,144,1..., dimensions={0} | all-to-all | bytes 1048576 | tf_op jit(solution)/shard_map/all_to_all | solution.py:233
  22.0 5.2 %attention.1 = (bf16[128,1024]{1,0:T(8,128)(2,1)}, f32[128,1024]{1,0:T(8,128)}, bf16[8,144,256]{2,1,0:T(8,128)(2,1)S(1)}) custom-call(s32[18]{0:T(128)S(1)} %pad_add_fusion.place, bf16[128,1024]{1,0:T(8,128)(2,1)S(1)} %bitcast.18, bf16[128,1024]{1,0:T(8,128)(2,1)S(1)} %bitcast.19, bf16[8,128,256]{2,1,0:T(8,128)(2,1)S(1)} %all_to_all.20.window, ...), custom_call_target="tpu_custom_call" | custom-call | flops 1610612736 | bytes 1048576 | tf_op jit(solution)/shard_map/attention/pallas_call | solution.py:141
  27.3 11.5 %all_to_all.21 = bf16[8,144,256]{2,1,0:T(8,128)(2,1)S(1)} all-to-all(bf16[8,144,256]{2,1,0:T(8,128)(2,1)S(1)} %get-tuple-element.20), channel_id=1, replica_groups={{56,0,8,16,24,32,40,48},{120,64,72,80,88,96,104,112},{184,128,136,144,1..., dimensions={0} | all-to-all | bytes 1179648 | tf_op jit(solution)/shard_map/all_to_all | solution.py:233
  38.8 0.3 fusion.1
  39.1 1.3 %collective-permute-start.1 = (bf16[128,256]{1,0:T(8,128)(2,1)S(1)}, bf16[128,256]{1,0:T(8,128)(2,1)S(1)}, u32[]{:S(2)}, u32[]{:S(2)}) collective-permute-start(bf16[128,256]{1,0:T(8,128)(2,1)S(1)} %get-tuple-element.24), channel_id=1, source_target_pairs={{64,0},{72,8},{80,16},{88,24},{96,32},{104,40},{112,48},{120,56},{... | collective-permute-start | bytes 196616 | tf_op jit(solution)/shard_map/ppermute | solution.py:208
  40.4 10.9 %all_to_all.22 = f32[8,4,384]{2,1,0:T(4,128)S(1)} all-to-all(f32[8,4,384]{2,1,0:T(4,128)S(1)} %broadcast_in_dim.76), channel_id=1, replica_groups={{7,0,1,2,3,4,5,6},{15,8,9,10,11,12,13,14},{23,16,17,18,19,20,21,22},{31..., dimensions={0} | all-to-all | bytes 98304 | tf_op jit(solution)/shard_map/all_to_all | solution.py:177
  51.3 0.0 collective-permute-done.1
  51.3 0.7 fusion.2
  52.0 21.3 %all_to_all.23 = f32[8,4,384]{2,1,0:T(4,128)S(1)} all-to-all(f32[8,4,384]{2,1,0:T(4,128)S(1)} %broadcast_in_dim.78), channel_id=1, replica_groups={{320,384,448,0,64,128,192,256},{328,392,456,8,72,136,200,264},{336,400,..., dimensions={0} | all-to-all | bytes 98304 | tf_op jit(solution)/shard_map/all_to_all | solution.py:240
  73.3 0.5 slice_bitcast_fusion.1
  73.8 0.6 copy.17
  (16 shorter events, 0.1 us)
Async XLA Ops:
  1.4 7.2 %collective-permute-start = (bf16[128,256]{1,0:T(8,128)(2,1)S(1)}, bf16[128,256]{1,0:T(8,128)(2,1)S(1)}, u32[]{:S(2)}, u32[]{:S(2)}) collective-permute-start(bf16[128,256]{1,0:T(8,128)(2,1)S(1)} %pad_maximum_fusion), channel_id=1, source_target_pairs={{0,64},{8,72},{16,80},{24,88},{32,96},{40,104},{48,112},{56,120},{... | collective-permute-start | bytes 196616 | tf_op jit(solution)/shard_map/ppermute | solution.py:192
  7.2 0.7 copy-start.2
  7.2 0.7 copy-start.3
  7.9 0.7 copy-start.4
  8.7 13.3 %copy-start = (bf16[1,128,1024]{2,1,0:T(8,128)(2,1)S(1)}, bf16[1,128,1024]{2,1,0:T(8,128)(2,1)}, u32[]{:S(2)}) copy-start(bf16[1,128,1024]{2,1,0:T(8,128)(2,1)} %param.7) | copy-start | bytes 786436
  8.7 13.3 %copy-start.1 = (bf16[1,128,1024]{2,1,0:T(8,128)(2,1)S(1)}, bf16[1,128,1024]{2,1,0:T(8,128)(2,1)}, u32[]{:S(2)}) copy-start(bf16[1,128,1024]{2,1,0:T(8,128)(2,1)} %param.10) | copy-start | bytes 786436
  39.1 12.2 %collective-permute-start.1 = (bf16[128,256]{1,0:T(8,128)(2,1)S(1)}, bf16[128,256]{1,0:T(8,128)(2,1)S(1)}, u32[]{:S(2)}, u32[]{:S(2)}) collective-permute-start(bf16[128,256]{1,0:T(8,128)(2,1)S(1)} %get-tuple-element.24), channel_id=1, source_target_pairs={{64,0},{72,8},{80,16},{88,24},{96,32},{104,40},{112,48},{120,56},{... | collective-permute-start | bytes 196616 | tf_op jit(solution)/shard_map/ppermute | solution.py:208

commit v6 on v5

--- a/solution.py
+++ b/solution.py
@@ -197,7 +197,8 @@
     attended, q_grad, partials = attention(place, queries[0], out_grad[0], window, bias)
 
     received = among_members(partials, groups)
-    sums = jnp.sum(received[:, tokens:].astype(f32), axis=0)
+    inverse = 1.0 / math.sqrt(groups * SPAN * tokens * lax.axis_size("rep"))
+    sums = jnp.sum(received[:, tokens:].astype(f32), axis=0) * inverse
     sums = sums[: SUM_ROWS // 2] + sums[SUM_ROWS // 2 :]
     full = width // (2 * head_dim)
     sums = jnp.concatenate([sums[:full], sums[full : 2 * full, :head_dim]], axis=1)
@@ -213,11 +214,8 @@
     rep_sums, k_grad, v_grad = lax.optimization_barrier((rep_sums, k_grad, v_grad))
     copies = jnp.broadcast_to(rep_sums[None], (groups,) + rep_sums.shape)
     rows = along_groups(copies, groups)
-    shards = groups * SPAN
-    inverse = 1.0 / math.sqrt(shards * tokens * lax.axis_size("rep"))
-    totals = jnp.sum(rows, axis=0) * inverse
-    q_total = totals[:, : 2 * head_dim].reshape(width)
-    v_total = totals[0, 2 * head_dim :]
+    q_total = jnp.sum(rows[:, :, : 2 * head_dim], axis=0).reshape(width)
+    v_total = jnp.sum(rows[:, 0, 2 * head_dim :], axis=0)
     return (
         attended[None],
         q_grad[None],

time: 74.8 us -> 74.8 us (level)
    unnamed x12 -> x11, local copies, waits for them, and re-layouts: 1.92 us -> 1.92 us
where the time goes in v6:
time: 74.8 us; the launch traced here: 74.4 us
  blocking collectives  56.9 us (76%)
  starting transfers between devices  7.01 us (9%)
  Pallas kernels  5.24 us (7%)
  other arithmetic  2.5 us (3%)
  local copies, waits for them, and re-layouts  1.95 us (3%)
  between operations  0.79 us (1%)
    all_to_all x2, blocking collectives, among_members(): lax.all_to_all(blocks, SEQ, 0, 0, axis_index_groups=[[g * SPAN + m for m...  24.8 us
    all_to_all x1, blocking collectives, along_groups(): lax.all_to_all(blocks, SEQ, 0, 0, axis_index_groups=[[g * SPAN + m for g...  21.3 us
    all_to_all x1, blocking collectives, exchanged(): lax.all_to_all(blocks, axis, 0, 0, axis_index_groups=rotated(lax.axis_siz...  10.9 us
    ppermute x1, starting transfers between devices, per_device(): lax.ppermute(own, SEQ, [(i, i + SPAN) for i in range((groups - 1) * SPAN)])  5.72 us
    pallas_call x1, Pallas kernels, attention(): pl.pallas_call(attention_kernel, out_shape=(jax.ShapeDtypeStruct((tokens,...  5.24 us
    unnamed x11, local copies, waits for them, and re-layouts  1.92 us
  transfers between devices with their start and end apart: 2, of which 0 were waited for; matrix products, arithmetic and copies ran while one was open for 0% of the time, Pallas kernels for 0%

profile of v6, /device:TPU:1, one launch (start us, length us, event | category | flops | bytes accessed | tf_op | source)
XLA Modules:
  0.0 74.4 jit_solution(8155493077702930427)
XLA Ops:
  0.6 0.8 %pad_maximum_fusion = bf16[128,256]{1,0:T(8,128)(2,1)S(1)} fusion(bf16[128,128]{1,0:T(8,128)(2,1)} %bitcast.18, bf16[128,128]{1,0:T(8,128)(2,1)} %bitcast.19), kind=kLoop, calls=%fused_computation.10 | loop fusion | flops 131072 | bytes 131072 | tf_op jit(solution)/shard_map/concatenate | solution.py:191
  1.4 5.7 %collective-permute-start = (bf16[128,256]{1,0:T(8,128)(2,1)S(1)}, bf16[128,256]{1,0:T(8,128)(2,1)S(1)}, u32[]{:S(2)}, u32[]{:S(2)}) collective-permute-start(bf16[128,256]{1,0:T(8,128)(2,1)S(1)} %pad_maximum_fusion), channel_id=1, source_target_pairs={{0,64},{8,72},{16,80},{24,88},{32,96},{40,104},{48,112},{56,120},{... | collective-permute-start | bytes 196616 | tf_op jit(solution)/shard_map/ppermute | solution.py:192
  7.2 0.0 copy-start.2
  7.2 0.0 copy-start.3
  7.2 0.6 copy-done.2
  7.8 0.0 copy-done.3
  7.9 0.0 copy-start.4
  7.9 0.6 copy-done.4
  8.5 0.1 pad_add_fusion.place
  8.6 0.0 collective-permute-done
  8.6 0.1 broadcast_select_fusion
  8.7 0.0 copy-start
  8.7 0.0 copy-start.1
  8.7 13.3 %all_to_all.20.window = bf16[8,128,256]{2,1,0:T(8,128)(2,1)S(1)} all-to-all(bf16[8,128,256]{2,1,0:T(8,128)(2,1)S(1)} %broadcast_select_fusion), channel_id=1, replica_groups={{56,0,8,16,24,32,40,48},{120,64,72,80,88,96,104,112},{184,128,136,144,1..., dimensions={0} | all-to-all | bytes 1048576 | tf_op jit(solution)/shard_map/all_to_all | solution.py:231
  22.0 5.2 %attention.1 = (bf16[128,1024]{1,0:T(8,128)(2,1)}, f32[128,1024]{1,0:T(8,128)}, bf16[8,144,256]{2,1,0:T(8,128)(2,1)S(1)}) custom-call(s32[18]{0:T(128)S(1)} %pad_add_fusion.place, bf16[128,1024]{1,0:T(8,128)(2,1)S(1)} %bitcast.16, bf16[128,1024]{1,0:T(8,128)(2,1)S(1)} %bitcast.17, bf16[8,128,256]{2,1,0:T(8,128)(2,1)S(1)} %all_to_all.20.window, ...), custom_call_target="tpu_custom_call" | custom-call | flops 1610612736 | bytes 1048576 | tf_op jit(solution)/shard_map/attention/pallas_call | solution.py:141
  27.3 11.5 %all_to_all.21 = bf16[8,144,256]{2,1,0:T(8,128)(2,1)S(1)} all-to-all(bf16[8,144,256]{2,1,0:T(8,128)(2,1)S(1)} %get-tuple-element.20), channel_id=1, replica_groups={{56,0,8,16,24,32,40,48},{120,64,72,80,88,96,104,112},{184,128,136,144,1..., dimensions={0} | all-to-all | bytes 1179648 | tf_op jit(solution)/shard_map/all_to_all | solution.py:231
  38.8 0.3 fusion.1
  39.1 1.3 %collective-permute-start.1 = (bf16[128,256]{1,0:T(8,128)(2,1)S(1)}, bf16[128,256]{1,0:T(8,128)(2,1)S(1)}, u32[]{:S(2)}, u32[]{:S(2)}) collective-permute-start(bf16[128,256]{1,0:T(8,128)(2,1)S(1)} %get-tuple-element.24), channel_id=1, source_target_pairs={{64,0},{72,8},{80,16},{88,24},{96,32},{104,40},{112,48},{120,56},{... | collective-permute-start | bytes 196616 | tf_op jit(solution)/shard_map/ppermute | solution.py:209
  40.4 10.9 %all_to_all.22 = f32[8,4,384]{2,1,0:T(4,128)S(1)} all-to-all(f32[8,4,384]{2,1,0:T(4,128)S(1)} %broadcast_in_dim.76), channel_id=1, replica_groups={{7,0,1,2,3,4,5,6},{15,8,9,10,11,12,13,14},{23,16,17,18,19,20,21,22},{31..., dimensions={0} | all-to-all | bytes 98304 | tf_op jit(solution)/shard_map/all_to_all | solution.py:177
  51.3 0.0 collective-permute-done.1
  51.3 0.7 fusion.2
  52.0 21.3 %all_to_all.23 = f32[8,4,384]{2,1,0:T(4,128)S(1)} all-to-all(f32[8,4,384]{2,1,0:T(4,128)S(1)} %broadcast_in_dim.78), channel_id=1, replica_groups={{320,384,448,0,64,128,192,256},{328,392,456,8,72,136,200,264},{336,400,..., dimensions={0} | all-to-all | bytes 98304 | tf_op jit(solution)/shard_map/all_to_all | solution.py:238
  73.3 0.6 copy.18
  73.9 0.5 reduce_sum.59
  (16 shorter events, 0.1 us)
Async XLA Ops:
  1.4 7.2 %collective-permute-start = (bf16[128,256]{1,0:T(8,128)(2,1)S(1)}, bf16[128,256]{1,0:T(8,128)(2,1)S(1)}, u32[]{:S(2)}, u32[]{:S(2)}) collective-permute-start(bf16[128,256]{1,0:T(8,128)(2,1)S(1)} %pad_maximum_fusion), channel_id=1, source_target_pairs={{0,64},{8,72},{16,80},{24,88},{32,96},{40,104},{48,112},{56,120},{... | collective-permute-start | bytes 196616 | tf_op jit(solution)/shard_map/ppermute | solution.py:192
  7.2 0.7 copy-start.2
  7.2 0.7 copy-start.3
  7.9 0.7 copy-start.4
  8.7 13.3 %copy-start = (bf16[1,128,1024]{2,1,0:T(8,128)(2,1)S(1)}, bf16[1,128,1024]{2,1,0:T(8,128)(2,1)}, u32[]{:S(2)}) copy-start(bf16[1,128,1024]{2,1,0:T(8,128)(2,1)} %param.7) | copy-start | bytes 786436
  8.7 13.3 %copy-start.1 = (bf16[1,128,1024]{2,1,0:T(8,128)(2,1)S(1)}, bf16[1,128,1024]{2,1,0:T(8,128)(2,1)}, u32[]{:S(2)}) copy-start(bf16[1,128,1024]{2,1,0:T(8,128)(2,1)} %param.10) | copy-start | bytes 786436
  39.1 12.2 %collective-permute-start.1 = (bf16[128,256]{1,0:T(8,128)(2,1)S(1)}, bf16[128,256]{1,0:T(8,128)(2,1)S(1)}, u32[]{:S(2)}, u32[]{:S(2)}) collective-permute-start(bf16[128,256]{1,0:T(8,128)(2,1)S(1)} %get-tuple-element.24), channel_id=1, source_target_pairs={{64,0},{72,8},{80,16},{88,24},{96,32},{104,40},{112,48},{120,56},{... | collective-permute-start | bytes 196616 | tf_op jit(solution)/shard_map/ppermute | solution.py:209

commit v7 on v6

--- a/solution.py
+++ b/solution.py
@@ -206,12 +206,12 @@
     received = received[:, :tokens].astype(f32)
     mine = jnp.sum(jnp.where(later, received, 0.0), axis=0)
     others = jnp.sum(jnp.where(later, 0.0, received), axis=0).astype(bf16)
+    copies, mine, others = lax.optimization_barrier((copies, mine, others))
+    rep_sums = jnp.sum(exchanged(copies, "rep", REP_FIRST), axis=0)
+    rep_sums, others = lax.optimization_barrier((rep_sums, others))
     returned = lax.ppermute(others, SEQ, [(i + SPAN, i) for i in range((groups - 1) * SPAN)])
-
-    rep_sums = jnp.sum(exchanged(copies, "rep", REP_FIRST), axis=0)
     k_grad = mine[None, :, :head_dim] + returned[None, :, :head_dim].astype(f32)
     v_grad = mine[None, :, head_dim:] + returned[None, :, head_dim:].astype(f32)
-    rep_sums, k_grad, v_grad = lax.optimization_barrier((rep_sums, k_grad, v_grad))
     copies = jnp.broadcast_to(rep_sums[None], (groups,) + rep_sums.shape)
     rows = along_groups(copies, groups)
     q_total = jnp.sum(rows[:, :, : 2 * head_dim], axis=0).reshape(width)

time: 74.8 us -> 75 us (level)
  blocking collectives: 56.9 us -> 35.6 us
  starting transfers between devices: 7.01 us -> 24.5 us
  waiting for transfers between devices: 0.01 us -> 3.02 us
    all_to_all x1 -> x0, blocking collectives: 21.3 us -> none  [along_groups(): lax.all_to_all(blocks, SEQ, 0, 0, axis_index_groups=[[g * SPAN + m for g...]
    all_to_all x0 -> x1, starting transfers between devices: none -> 17.5 us  [along_groups(): lax.all_to_all(blocks, SEQ, 0, 0, axis_index_groups=[[g * SPAN + m for g...]
    all_to_all x0 -> x1, waiting for transfers between devices: none -> 3.02 us  [along_groups(): lax.all_to_all(blocks, SEQ, 0, 0, axis_index_groups=[[g * SPAN + m for g...]
  transfers between devices with their start and end apart: 2 -> 3, of which waited for: 0 -> 1; matrix products, arithmetic and copies ran while one was open for 0% -> 2% of each run, Pallas kernels for 0% -> 0%
where the time goes in v7:
time: 75 us; the launch traced here: 74.3 us
  blocking collectives  35.6 us (47%)
  starting transfers between devices  24.5 us (33%)
  Pallas kernels  5.24 us (7%)
  waiting for transfers between devices  3.02 us (4%)
  local copies, waits for them, and re-layouts  2.57 us (3%)
  other arithmetic  2.5 us (3%)
  between operations  0.78 us (1%)
    all_to_all x2, blocking collectives, among_members(): lax.all_to_all(blocks, SEQ, 0, 0, axis_index_groups=[[g * SPAN + m for m...  24.8 us
    all_to_all x1, starting transfers between devices, along_groups(): lax.all_to_all(blocks, SEQ, 0, 0, axis_index_groups=[[g * SPAN + m for g...  17.5 us
    all_to_all x1, blocking collectives, exchanged(): lax.all_to_all(blocks, axis, 0, 0, axis_index_groups=rotated(lax.axis_siz...  10.9 us
    ppermute x1, starting transfers between devices, per_device(): lax.ppermute(own, SEQ, [(i, i + SPAN) for i in range((groups - 1) * SPAN)])  5.72 us
    pallas_call x1, Pallas kernels, attention(): pl.pallas_call(attention_kernel, out_shape=(jax.ShapeDtypeStruct((tokens,...  5.24 us
    all_to_all x1, waiting for transfers between devices, along_groups(): lax.all_to_all(blocks, SEQ, 0, 0, axis_index_groups=[[g * SPAN + m for g...  3.02 us
    unnamed x11, local copies, waits for them, and re-layouts  1.92 us
  transfers between devices with their start and end apart: 3, of which 1 were waited for; matrix products, arithmetic and copies ran while one was open for 2% of the time, Pallas kernels for 0%

profile of v7, /device:TPU:1, one launch (start us, length us, event | category | flops | bytes accessed | tf_op | source)
XLA Modules:
  0.0 74.3 jit_solution(3085233017231917750)
XLA Ops:
  0.6 0.8 %pad_maximum_fusion = bf16[128,256]{1,0:T(8,128)(2,1)S(1)} fusion(bf16[128,128]{1,0:T(8,128)(2,1)} %bitcast.18, bf16[128,128]{1,0:T(8,128)(2,1)} %bitcast.19), kind=kLoop, calls=%fused_computation.6 | loop fusion | flops 131072 | bytes 131072 | tf_op jit(solution)/shard_map/concatenate | solution.py:191
  1.4 5.7 %collective-permute-start = (bf16[128,256]{1,0:T(8,128)(2,1)S(1)}, bf16[128,256]{1,0:T(8,128)(2,1)S(1)}, u32[]{:S(2)}, u32[]{:S(2)}) collective-permute-start(bf16[128,256]{1,0:T(8,128)(2,1)S(1)} %pad_maximum_fusion), channel_id=1, source_target_pairs={{0,64},{8,72},{16,80},{24,88},{32,96},{40,104},{48,112},{56,120},{... | collective-permute-start | bytes 196616 | tf_op jit(solution)/shard_map/ppermute | solution.py:192
  7.2 0.0 copy-start.2
  7.2 0.0 copy-start.3
  7.2 0.6 copy-done.2
  7.9 0.0 copy-start.4
  7.9 0.6 copy-done.4
  8.5 0.1 pad_add_fusion.place
  8.6 0.0 collective-permute-done
  8.6 0.1 broadcast_select_fusion
  8.7 0.0 copy-start
  8.7 0.0 copy-start.1
  8.7 13.3 %all_to_all.20.window = bf16[8,128,256]{2,1,0:T(8,128)(2,1)S(1)} all-to-all(bf16[8,128,256]{2,1,0:T(8,128)(2,1)S(1)} %broadcast_select_fusion), channel_id=1, replica_groups={{56,0,8,16,24,32,40,48},{120,64,72,80,88,96,104,112},{184,128,136,144,1..., dimensions={0} | all-to-all | bytes 1048576 | tf_op jit(solution)/shard_map/all_to_all | solution.py:231
  22.0 5.2 %attention.1 = (bf16[128,1024]{1,0:T(8,128)(2,1)}, f32[128,1024]{1,0:T(8,128)}, bf16[8,144,256]{2,1,0:T(8,128)(2,1)S(1)}) custom-call(s32[18]{0:T(128)S(1)} %pad_add_fusion.place, bf16[128,1024]{1,0:T(8,128)(2,1)S(1)} %bitcast.16, bf16[128,1024]{1,0:T(8,128)(2,1)S(1)} %bitcast.17, bf16[8,128,256]{2,1,0:T(8,128)(2,1)S(1)} %all_to_all.20.window, ...), custom_call_target="tpu_custom_call" | custom-call | flops 1610612736 | bytes 1048576 | tf_op jit(solution)/shard_map/attention/pallas_call | solution.py:141
  27.3 11.5 %all_to_all.21 = bf16[8,144,256]{2,1,0:T(8,128)(2,1)S(1)} all-to-all(bf16[8,144,256]{2,1,0:T(8,128)(2,1)S(1)} %get-tuple-element.22), channel_id=1, replica_groups={{56,0,8,16,24,32,40,48},{120,64,72,80,88,96,104,112},{184,128,136,144,1..., dimensions={0} | all-to-all | bytes 1179648 | tf_op jit(solution)/shard_map/all_to_all | solution.py:231
  38.8 0.3 fusion.1
  39.1 10.9 %all_to_all.22 = f32[8,4,384]{2,1,0:T(4,128)S(1)} all-to-all(f32[8,4,384]{2,1,0:T(4,128)S(1)} %broadcast_in_dim.76), channel_id=1, replica_groups={{7,0,1,2,3,4,5,6},{15,8,9,10,11,12,13,14},{23,16,17,18,19,20,21,22},{31..., dimensions={0} | all-to-all | bytes 98304 | tf_op jit(solution)/shard_map/all_to_all | solution.py:177
  50.0 1.3 %collective-permute-start.1 = (bf16[128,256]{1,0:T(8,128)(2,1)S(1)}, bf16[128,256]{1,0:T(8,128)(2,1)S(1)}, u32[]{:S(2)}, u32[]{:S(2)}) collective-permute-start(bf16[128,256]{1,0:T(8,128)(2,1)S(1)} %get-tuple-element.26), channel_id=1, source_target_pairs={{64,0},{72,8},{80,16},{88,24},{96,32},{104,40},{112,48},{120,56},{... | collective-permute-start | bytes 196616 | tf_op jit(solution)/shard_map/ppermute | solution.py:212
  51.3 0.6 broadcast_in_dim.78
  51.9 17.5 %all-to-all-start.3 = ((f32[8,4,384]{2,1,0:T(4,128)}), f32[8,4,384]{2,1,0:T(4,128)S(1)}, u32[]{:S(2)}, u32[]{:S(2)}) async-start(f32[8,4,384]{2,1,0:T(4,128)} %broadcast_in_dim.78), calls=%async_computation.3 | async-start | bytes 98304 | tf_op jit(solution)/shard_map/all_to_all | solution.py:238
  69.5 0.7 add_bitcast_fusion
  70.1 3.0 %all-to-all-done.3 = f32[8,4,384]{2,1,0:T(4,128)S(1)} async-done(((f32[8,4,384]{2,1,0:T(4,128)}), f32[8,4,384]{2,1,0:T(4,128)S(1)}, u32[]{:S(2)}, u32[]{:S(2)}) %all-to-all-start.3) | async-done | bytes 49184 | tf_op jit(solution)/shard_map/all_to_all | solution.py:238
  73.2 0.6 copy.18
  73.8 0.5 reduce_sum.59
  (17 shorter events, 0.1 us)
Async XLA Ops:
  1.4 7.2 %collective-permute-start = (bf16[128,256]{1,0:T(8,128)(2,1)S(1)}, bf16[128,256]{1,0:T(8,128)(2,1)S(1)}, u32[]{:S(2)}, u32[]{:S(2)}) collective-permute-start(bf16[128,256]{1,0:T(8,128)(2,1)S(1)} %pad_maximum_fusion), channel_id=1, source_target_pairs={{0,64},{8,72},{16,80},{24,88},{32,96},{40,104},{48,112},{56,120},{... | collective-permute-start | bytes 196616 | tf_op jit(solution)/shard_map/ppermute | solution.py:192
  7.2 0.7 copy-start.2
  7.2 0.7 copy-start.3
  7.9 0.7 copy-start.4
  8.7 13.3 %copy-start = (bf16[1,128,1024]{2,1,0:T(8,128)(2,1)S(1)}, bf16[1,128,1024]{2,1,0:T(8,128)(2,1)}, u32[]{:S(2)}) copy-start(bf16[1,128,1024]{2,1,0:T(8,128)(2,1)} %param.7) | copy-start | bytes 786436
  8.7 13.3 %copy-start.1 = (bf16[1,128,1024]{2,1,0:T(8,128)(2,1)S(1)}, bf16[1,128,1024]{2,1,0:T(8,128)(2,1)}, u32[]{:S(2)}) copy-start(bf16[1,128,1024]{2,1,0:T(8,128)(2,1)} %param.10) | copy-start | bytes 786436
  50.0 19.5 %collective-permute-start.1 = (bf16[128,256]{1,0:T(8,128)(2,1)S(1)}, bf16[128,256]{1,0:T(8,128)(2,1)S(1)}, u32[]{:S(2)}, u32[]{:S(2)}) collective-permute-start(bf16[128,256]{1,0:T(8,128)(2,1)S(1)} %get-tuple-element.26), channel_id=1, source_target_pairs={{64,0},{72,8},{80,16},{88,24},{96,32},{104,40},{112,48},{120,56},{... | collective-permute-start | bytes 196616 | tf_op jit(solution)/shard_map/ppermute | solution.py:212
  51.9 21.2 %all-to-all-start.3 = ((f32[8,4,384]{2,1,0:T(4,128)}), f32[8,4,384]{2,1,0:T(4,128)S(1)}, u32[]{:S(2)}, u32[]{:S(2)}) async-start(f32[8,4,384]{2,1,0:T(4,128)} %broadcast_in_dim.78), calls=%async_computation.3 | async-start | bytes 98304 | tf_op jit(solution)/shard_map/all_to_all | solution.py:238
